TPU v7x, 128 devices: a whole 4x4x4 slice. The times are simulated.
128 devices in a mesh: dp: 2 (over z_lo), ctx: 8 (over x, core), tensor: 8 (over z_hi, y).
Axes of the slice: x: 4, y: 4, z: 4 (z_hi: 2, z_lo: 2; z = z_hi * 2 + z_lo), core: 2. Of those that a mesh axis runs over, the one named last changes fastest.
Arguments:
- tokens: bfloat16 [8192, 8192], P(('dp', 'ctx'), 'tensor'), may hold values from -6 to 6
- norm_gain: float32 [8192], replicated, may hold values from 0.5 to 14
- project_weight: bfloat16 [8192, 8, 768], P(None, 'tensor'), may hold values from -0.0625 to 0.0625
- project_bias: bfloat16 [8, 768], P('tensor'), may hold values from -3 to 3
- output_weight: bfloat16 [4096, 8192], P('tensor'), may hold values from -0.09375 to 0.09375
- source_row: int32 [8192], P(('dp', 'ctx')), may hold values from 0 to 8191, as said below
- segment_id: int32 [8192], P(('dp', 'ctx')), may hold values from 0 to 11, as said below
Outputs:
- sublayer_out: bfloat16 [8192, 8192], P(('dp', 'ctx', 'tensor'))
Inputs may be any that keep to these rules, and one draw needn't show every extreme that they name: `source_row`: A permutation of the rollout rows; each document moves as one run in its order. `segment_id`: each packed sequence of 4096 positions holds exactly 6 documents, each a run of equal ids; ids differ between packed sequences.
All inputs are finite; a program needn't handle non-finite values.
Results may differ from a plain program's by a relative error of at most 0.023.
The roundings to bfloat16 on the way count: a program that leaves them out, or rounds other values in their place, can miss the bound.
Values may be sent and summed in bfloat16 or wider, within the bound.
A program may use at most 128 MiB of HBM per device.

v0:
```python
import jax
import jax.numpy as jnp
from jax import lax
from jax.sharding import PartitionSpec as P

HD = 128
GROUP = 4


def angle_tables(positions):
    half_size = HD // 2
    freqs = 1000000.0 ** (-(jnp.arange(half_size, dtype=jnp.float32) * 2.0) / HD)
    angles = positions.astype(jnp.float32)[:, None] * freqs[None, :]
    return (jnp.cos(angles), jnp.sin(angles))


def rotate_pairs(values, cosine, sine_part):
    half_size = HD // 2
    first_half = values[..., :half_size]
    second_half = values[..., half_size:]
    return jnp.concatenate(
        [
            first_half * cosine - second_half * sine_part,
            second_half * cosine + first_half * sine_part,
        ],
        axis=-1,
    )


def per_device(
    tokens, norm_gain, project_weight, project_bias, output_weight, source_row, segment_id
):
    local_rows = tokens.shape[0]
    first_row = lax.axis_index(("dp", "ctx")) * local_rows
    kv_heads = project_weight.shape[1]
    slot_width = project_weight.shape[2]
    flat_weight = project_weight.reshape(project_weight.shape[0], kv_heads * slot_width)
    flat_bias = project_bias.reshape(-1).astype(jnp.float32)
    shard_piece = lax.all_gather(tokens, ("dp", "ctx"), axis=0, tiled=True)
    length = shard_piece.shape[0]
    within = source_row
    inside = (within >= 0) & (within < length)
    taken = jnp.take(shard_piece, jnp.clip(within, 0, length - 1), axis=0)
    packed = jnp.where(inside[:, None], taken, jnp.zeros(tokens.shape, tokens.dtype))
    features = lax.all_gather(packed, "tensor", axis=1, tiled=True)
    wide = features.astype(jnp.float32)
    meansq = jnp.mean(wide * wide, axis=-1, keepdims=True)
    normed = (wide * lax.rsqrt(meansq + 1e-06) * norm_gain).astype(jnp.bfloat16)
    projected = (
        jnp.dot(normed, flat_weight, preferred_element_type=jnp.float32) + flat_bias
    ).astype(jnp.bfloat16)
    stacked = (
        lax.optimization_barrier(projected)
        .astype(jnp.float32)
        .reshape(local_rows, kv_heads, GROUP + 2, HD)
    )
    positions = lax.axis_index("ctx") * local_rows + jnp.arange(local_rows, dtype=jnp.int32)
    cosine, sine_part = angle_tables(positions)
    queries = rotate_pairs(
        stacked[:, :, :GROUP], cosine[:, None, None], sine_part[:, None, None]
    ).astype(jnp.bfloat16)
    keys_rot = rotate_pairs(stacked[:, :, GROUP], cosine[:, None], sine_part[:, None]).astype(
        jnp.bfloat16
    )
    values = projected.reshape(local_rows, kv_heads, GROUP + 2, HD)[:, :, GROUP + 1]
    query_mat = queries.transpose(1, 2, 0, 3).reshape(kv_heads, GROUP * local_rows, HD)
    query_pos = jnp.tile(positions, GROUP)
    query_seg = jnp.tile(segment_id, GROUP)
    score_scale = HD ** (-0.5)
    running_max = jnp.full((kv_heads, GROUP * local_rows), -1e30, jnp.float32)
    key_piece = lax.all_gather(keys_rot, "ctx", axis=0, tiled=True)
    value_piece = lax.all_gather(values, "ctx", axis=0, tiled=True)
    seg_piece = lax.all_gather(segment_id, "ctx", axis=0, tiled=True)
    length = key_piece.shape[0]
    key_pos = jnp.arange(length, dtype=jnp.int32)
    scores = (
        jnp.einsum("hqd,khd->hqk", query_mat, key_piece, preferred_element_type=jnp.float32)
        * score_scale
    )
    allowed = (query_seg[:, None] == seg_piece[None, :]) & (key_pos[None, :] <= query_pos[:, None])
    scores = jnp.where(allowed[None], scores, -1e30)
    new_max = jnp.maximum(running_max, jnp.max(scores, axis=-1))
    weights = jnp.where(allowed[None], jnp.exp(scores - new_max[..., None]), 0.0)
    denominator = jnp.sum(weights, axis=-1)
    weighted = jnp.einsum(
        "hqk,khd->hqd", weights, value_piece.astype(jnp.float32), precision=lax.Precision.HIGHEST
    )
    attended = (
        (weighted / denominator[..., None])
        .reshape(kv_heads, GROUP, local_rows, HD)
        .transpose(2, 0, 1, 3)
        .reshape(local_rows, -1)
        .astype(jnp.bfloat16)
    )
    value_rows = lax.all_gather(attended, ("dp", "ctx"), axis=0, tiled=True)
    targets = lax.all_gather(source_row, ("dp", "ctx"), axis=0, tiled=True)
    within = targets - first_row
    within = jnp.where((within >= 0) & (within < local_rows), within, local_rows)
    unpacked = jnp.zeros_like(attended).at[within].set(value_rows, mode="drop")
    summed = lax.psum_scatter(
        jnp.dot(unpacked, output_weight, preferred_element_type=jnp.float32).astype(jnp.bfloat16),
        "tensor",
        scatter_dimension=0,
        tiled=True,
    )
    return summed


def solution(mesh):
    placed = (
        P(("dp", "ctx"), "tensor"),
        P(),
        P(None, "tensor", None),
        P("tensor", None),
        P("tensor", None),
        P(("dp", "ctx")),
        P(("dp", "ctx")),
    )
    return jax.shard_map(
        per_device,
        mesh=mesh,
        in_specs=placed,
        out_specs=P(("dp", "ctx", "tensor"), None),
        check_vma=False,
    )
```

profile of v0, /device:TPU:32, one launch (start us, length us, event | category | flops | bytes accessed | tf_op | source)
XLA Modules:
  0.0 558.9 jit_solution(10945706907007343198)
XLA Ops:
  6.5 0.7 all-gather.9.cloned.1.call-update
  7.3 0.7 compare_select_fusion.1
  8.0 0.7 compare_and_fusion.1
  8.7 94.0 %all-gather.9.cloned.1.call-done = bf16[8192,1024]{1,0:T(8,128)(2,1)} async-done(((bf16[512,1024]{1,0:T(8,128)(2,1)}), bf16[8192,1024]{1,0:T(8,128)(2,1)}) %all-gather.9.cloned.1.call-update) | async-done | bytes 16777232 | tf_op jit(solution)/shard_map/all_gather | solution.py:39
  102.7 10.7 %gather_fusion = bf16[512,1024]{1,0:T(8,128)(2,1)S(1)} fusion(bf16[8192,1024]{1,0:T(8,128)(2,1)} %all-gather.9.cloned.1.call-done, s32[1024]{0:T(1024)S(1)} %pad_clamp_fusion), kind=kCustom, calls=%fused_computation | custom fusion | bytes 2099200 | tf_op jit(solution)/shard_map/jit(_take)/gather | solution.py:43
  113.4 1.2 select_select_fusion
  114.7 0.7 convert_reduce_fusion
  115.4 108.2 %all-gather.11.cloned.1.call-done = bf16[512,8192]{1,0:T(8,128)(2,1)} async-done(((bf16[512,1024]{1,0:T(8,128)(2,1)}), bf16[512,8192]{1,0:T(8,128)(2,1)}) %all-gather.11.cloned.1.call-update) | async-done | bytes 8388624 | tf_op jit(solution)/shard_map/all_gather | solution.py:45
  223.6 5.1 fusion.4
  228.7 12.9 %add_convert_fusion = bf16[512,768]{1,0:T(8,128)(2,1)S(1)} fusion(bf16[8192,1,768]{2,0,1:T(8,128)(2,1)} %param.9, bf16[512,8192]{1,0:T(8,128)(2,1)} %all-gather.11.cloned.1.call-done, f32[8192]{0:T(1024)S(1)} %copy-done.2, f32[512]{0:T(512)S(1)} %add_rsqrt_fusion, f32[768]{0:T(1024)S(1)} %convert_reduce_fusion), kind=kOutput, calls=%fused_computation.28 | convolution fusion | flops 6460014592 | bytes 21795840 | tf_op jit(solution)/shard_map/dot_general | solution.py:50
  242.5 0.7 pad_maximum_fusion
  243.3 11.9 %all-gather.2 = s32[8,1,512]{2,1,0:T(1,128)S(1)} all-gather(s32[1,1,512]{2,1,0:T(1,128)S(1)} %bitcast.58), channel_id=1, replica_groups=mesh['dp'=2,'ctx'=8,'tensor'=8] {'ctx'}, dimensions={0}, use_global_device_ids=true | all-gather | bytes 18432 | tf_op jit(solution)/shard_map/all_gather | solution.py:73
  256.5 0.7 slice.34
  257.4 7.8 %all-gather.13.cloned.1.call-done = bf16[4096,1,128]{0,2,1:T(8,128)(2,1)} async-done(((bf16[512,1,128]{0,2,1:T(8,128)(2,1)}), bf16[4096,1,128]{0,2,1:T(8,128)(2,1)}) %all-gather.13.cloned.1.call-update) | async-done | bytes 1048592 | tf_op jit(solution)/shard_map/all_gather | solution.py:71
  265.3 15.3 %fusion.1 = (f32[2048]{0:T(1024)S(1)}, f32[2048,4096]{1,0:T(8,128)}) fusion(s32[2048]{0:T(1024)S(1)} %bitcast.51, s32[4096]{0:T(1024)S(1)} %bitcast.48, s32[2048]{0:T(1024)S(1)} %bitcast.54, bf16[2048,128]{1,0:T(8,128)(2,1)S(1)} %bitcast.44, bf16[4096,1,128]{0,2,1:T(8,128)(2,1)} %all-gather.13.cloned.1.call-done), kind=kOutput, calls=%fused_computation.6 | convolution fusion | flops 2197813248 | bytes 35168256 | tf_op jit(solution)/shard_map/hqd,khd->hqk/dot_general | solution.py:77
  280.5 16.9 %fusion.2 = f32[2048]{0:T(1024)S(1)} fusion(f32[2048,4096]{1,0:T(8,128)} %get-tuple-element.14, f32[2048]{0:T(1024)S(1)} %broadcast_maximum_fusion, s32[2048]{0:T(1024)S(1)} %bitcast.52, s32[4096]{0:T(1024)S(1)} %bitcast.49, s32[2048]{0:T(1024)S(1)} %bitcast.55), kind=kLoop, calls=%fused_computation.9 | loop fusion | flops 67106816 | bytes 33603584 | tf_op jit(solution)/shard_map/reduce_sum | solution.py:84
  297.4 28.7 %fusion.20 = bf16[2048,128]{1,0:T(8,128)(2,1)S(1)} fusion(f32[2048,4096]{1,0:T(8,128)} %get-tuple-element.14, f32[2048]{0:T(1024)S(1)} %broadcast_maximum_fusion, s32[2048]{0:T(1024)S(1)} %bitcast.53, s32[4096]{0:T(1024)S(1)} %bitcast.50, s32[2048]{0:T(1024)S(1)} %bitcast.56, bf16[4096,1,1,128]{0,3,2,1:T(8,128)(2,1)} %all-gather.17.cloned.1.call-done, ...), kind=kOutput, calls=%fused_computation.27 | convolution fusion | flops 12944146432 | bytes 35176448 | tf_op jit(solution)/shard_map/hqk,khd->hqd/dot_general | solution.py:85
  326.1 1.0 copy.23
  327.2 17.4 %all-gather.1 = s32[16,1,512]{2,1,0:T(1,128)S(1)} all-gather(s32[1,1,512]{2,1,0:T(1,128)S(1)} %bitcast.57), channel_id=1, replica_groups=mesh['dp'=2,'ctx'=8,'tensor'=8] {'dp','ctx'}, dimensions={0}, use_global_device_ids=true | all-gather | bytes 34816 | tf_op jit(solution)/shard_map/all_gather | solution.py:96
  344.6 34.6 %all-gather.15.cloned.1.call-done = bf16[8192,512]{0,1:T(8,128)(2,1)} async-done(((bf16[512,512]{0,1:T(8,128)(2,1)}), bf16[8192,512]{0,1:T(8,128)(2,1)}) %all-gather.15.cloned.1.call-update) | async-done | bytes 8388624 | tf_op jit(solution)/shard_map/all_gather | solution.py:95
  379.3 11.9 %copy.24 = bf16[8192,512]{1,0:T(8,128)(2,1)} copy(bf16[8192,512]{0,1:T(8,128)(2,1)} %all-gather.15.cloned.1.call-done) | data formatting | bytes 16777216 | tf_op jit(solution)/shard_map/all_gather | solution.py:95
  391.2 35.9 %scatter_custom_fusion = bf16[512,512]{1,0:T(8,128)(2,1)S(1)} fusion(s32[8192]{0:T(1024)S(1)} %compare_select_fusion, bf16[8192,512]{1,0:T(8,128)(2,1)} %copy.24, bf16[]{:T(256)} %constant.20.clone.1), kind=kCustom, calls=%fused_computation.37 | custom fusion | bytes 524800 | tf_op jit(solution)/shard_map/scatter | solution.py:99
  427.1 10.1 %convolution_convert_fusion = bf16[512,8192]{1,0:T(8,128)(2,1)} fusion(bf16[512,512]{1,0:T(8,128)(2,1)S(1)} %scatter_custom_fusion, bf16[512,8192]{1,0:T(8,128)(2,1)} %param.11), kind=kOutput, calls=%fused_computation.23 | convolution fusion | flops 4299161600 | bytes 17301504 | tf_op jit(solution)/shard_map/dot_general | solution.py:101
  437.2 114.8 %reduce-scatter.2.cloned.1.call-done = bf16[64,8192]{1,0:T(8,128)(2,1)} async-done(((bf16[512,8192]{1,0:T(8,128)(2,1)}), bf16[64,8192]{1,0:T(8,128)(2,1)}) %reduce-scatter.2.cloned.1.call-update) | async-done | bytes 1048592 | tf_op jit(solution)/shard_map/reduce_scatter | solution.py:100
  (37 shorter events, 2.7 us)
Async XLA Ops:
  6.5 222.2 %copy-start.2 = (f32[8192]{0:T(1024)S(1)}, f32[8192]{0:T(1024)}, u32[]{:S(2)}) copy-start(f32[8192]{0:T(1024)} %param.8) | copy-start | bytes 98308
  6.5 96.2 %all-gather.9.cloned.1.call-start = ((), (), s32[]{:S(2)}) async-start(), calls=%async_computation.1 | async-start | bytes 17825792 | tf_op jit(solution)/shard_map/all_gather | solution.py:39
  7.3 216.3 %all-gather.11.cloned.1.call-start = ((), (), s32[]{:S(2)}) async-start(), calls=%async_computation.2 | async-start | bytes 9437184 | tf_op jit(solution)/shard_map/all_gather | solution.py:45
  114.6 150.7 %all-gather.13.cloned.1.call-start = ((), (), s32[]{:S(2)}) async-start(), calls=%async_computation.3 | async-start | bytes 1179648 | tf_op jit(solution)/shard_map/all_gather | solution.py:71
  228.7 14.6 %copy-start.1 = (s32[512]{0:T(512)S(1)}, s32[512]{0:T(512)}, u32[]{:S(2)}) copy-start(s32[512]{0:T(512)} %param.13) | copy-start | bytes 6148
  243.2 54.2 %all-gather.17.cloned.1.call-start = ((), (), s32[]{:S(2)}) async-start(), calls=%async_computation.6 | async-start | bytes 1179648 | tf_op jit(solution)/shard_map/all_gather | solution.py:72
  257.2 122.1 %all-gather.15.cloned.1.call-start = ((), (), s32[]{:S(2)}) async-start(), calls=%async_computation.4 | async-start | bytes 8912896 | tf_op jit(solution)/shard_map/all_gather | solution.py:95
  297.4 29.8 %copy-start = (s32[512]{0:T(512)S(1)}, s32[512]{0:T(512)}, u32[]{:S(2)}) copy-start(s32[512]{0:T(512)} %param.12) | copy-start | bytes 6148
  327.2 224.9 %reduce-scatter.2.cloned.1.call-start = ((), (), s32[]{:S(2)}) async-start(), calls=%async_computation.5 | async-start | bytes 9437184 | tf_op jit(solution)/shard_map/reduce_scatter | solution.py:100
Sparse Core Ops, SparseCore 0:
  9.1 93.5 all-gather.8
  114.7 108.8 all-gather.10
  243.3 21.8 all-gather.12
  266.8 23.1 all-gather.16
  327.3 51.9 all-gather.14
  437.4 114.6 reduce-scatter.1
where the time goes:
time: 561 us; the launch traced here: 559 us
  waiting for transfers between devices  360 us (64%)
  matrix products  67 us (12%)
  local copies, waits for them, and re-layouts  61 us (11%)
  blocking collectives  29.2 us (5%)
  other arithmetic  27.3 us (5%)
  between operations  13.7 us (2%)
    reduce_scatter x1, waiting for transfers between devices, per_device(): lax.psum_scatter(jnp.dot(unpacked, output_weight, preferred_element_type=...  115 us
    all_gather x1, waiting for transfers between devices, per_device(): features = lax.all_gather(packed, 'tensor', axis=1, tiled=True)  108 us
    all_gather x1, waiting for transfers between devices, per_device(): shard_piece = lax.all_gather(tokens, ('dp', 'ctx'), axis=0, tiled=True)  94 us
    scatter x1, local copies, waits for them, and re-layouts, per_device(): unpacked = jnp.zeros_like(attended).at[within].set(value_rows, mode='drop')  35.9 us
    all_gather x1, waiting for transfers between devices, per_device(): value_rows = lax.all_gather(attended, ('dp', 'ctx'), axis=0, tiled=True)  34.6 us
    dot_general x1, matrix products, per_device(): jnp.einsum('hqk,khd->hqd', weights, value_piece.astype(jnp.float32), prec...  28.7 us
    all_gather x1, blocking collectives, per_device(): targets = lax.all_gather(source_row, ('dp', 'ctx'), axis=0, tiled=True)  17.4 us
    reduce_sum x1, other arithmetic, per_device(): denominator = jnp.sum(weights, axis=-1)  16.9 us
  transfers between devices with their start and end apart: 6, of which 5 were waited for; matrix products, arithmetic and copies ran while one was open for 6% of the time, Pallas kernels for 0%

commit v1 on v0

v1 whole, which is shorter than its diff:
```python
import functools

import jax
import jax.numpy as jnp
from jax import lax
from jax.experimental import pallas as pl
from jax.experimental.pallas import tpu as pltpu
from jax.sharding import PartitionSpec as P

HD = 128
GROUP = 4
PACK = 4096
DOC_IDS = 12
N_T = 8
SUBS = 4
MESH = pl.DeviceIdType.MESH
VMEM = pltpu.VMEM
DMA = pltpu.SemaphoreType.DMA


def peer(index):
    return {"tensor": index}


def greet(others):
    barrier = pltpu.get_barrier_semaphore()
    for other in others:
        pl.semaphore_signal(barrier, inc=1, device_id=peer(other), device_id_type=MESH)


def greeted(count):
    pl.semaphore_wait(pltpu.get_barrier_semaphore(), count)


def remote(src, dst, send_sem, recv_sem, to):
    return pltpu.make_async_remote_copy(
        src_ref=src,
        dst_ref=dst,
        send_sem=send_sem,
        recv_sem=recv_sem,
        device_id=peer(to),
        device_id_type=MESH,
    )


def all_others(me):
    return [lax.rem(me + d, N_T) for d in range(1, N_T)]


def norm_kernel(
    features,
    tok_ref,
    gain_ref,
    wo_ref,
    normed_ref,
    shuffled_ref,
    stats,
    stat_send,
    stat_recv,
    w_send,
    w_recv,
    own_sem,
):
    me = lax.axis_index("tensor")
    replica = lax.axis_index("dp") * lax.axis_size("ctx") + lax.axis_index("ctx")
    rows, width = tok_ref.shape
    piece, columns = shuffled_ref.shape[1:]
    others = all_others(me)
    greet(others)
    block = 128
    for i in range(rows // block):
        total = jnp.zeros((block, 128), jnp.float32)
        for j in range(width // 128):
            part = tok_ref[i * block : (i + 1) * block, j * 128 : (j + 1) * 128].astype(jnp.float32)
            total = total + part * part
        summed = jnp.sum(total.T, axis=0, keepdims=True)
        stats[pl.ds(me, 1), :, i * block : (i + 1) * block] = jnp.broadcast_to(
            summed[None], (1, 8, block)
        )
    greeted(N_T - 1)
    mine = pl.ds(pl.multiple_of(replica * piece, piece), piece)

    def columns_of(index):
        return pl.ds(pl.multiple_of(index * columns, columns), columns)

    stat_copies = []
    w_copies = []
    for d, other in enumerate(others):
        copy = remote(
            stats.at[me], stats.at[me], stat_send.at[d], stat_recv.at[d], other
        )
        copy.start()
        stat_copies.append(copy)
    for d, other in enumerate(others):
        copy = remote(
            wo_ref.at[mine, columns_of(other)],
            shuffled_ref.at[me],
            w_send.at[d],
            w_recv.at[d],
            other,
        )
        copy.start()
        w_copies.append(copy)
    own = pltpu.make_async_copy(wo_ref.at[mine, columns_of(me)], shuffled_ref.at[me], own_sem)
    own.start()
    for copy in stat_copies:
        copy.wait()
    summed = stats[0]
    for t in range(1, N_T):
        summed = summed + stats[t]
    scale = lax.rsqrt(summed[0:1] * (1.0 / features) + 1e-06)
    for i in range(rows // block):
        along = jnp.broadcast_to(scale[:, i * block : (i + 1) * block], (128, block)).T
        for j in range(width // 128):
            cut = (slice(i * block, (i + 1) * block), slice(j * 128, (j + 1) * 128))
            gain = gain_ref[me, :, j * 128 : (j + 1) * 128]
            normed_ref[cut] = (tok_ref[cut].astype(jnp.float32) * along * gain).astype(jnp.bfloat16)
    own.wait()
    for copy in w_copies:
        copy.wait()


def normalise(tokens, gain, out_weight, replicas):
    rows, width = tokens.shape
    depth, out_width = out_weight.shape
    piece, columns = depth // replicas, out_width // N_T
    return pl.pallas_call(
        functools.partial(norm_kernel, width * N_T),
        out_shape=(
            jax.ShapeDtypeStruct((rows, width), jnp.bfloat16),
            jax.ShapeDtypeStruct((N_T, piece, columns), jnp.bfloat16),
        ),
        in_specs=[
            pl.BlockSpec(memory_space=VMEM),
            pl.BlockSpec(memory_space=VMEM),
            pl.BlockSpec(memory_space=pl.ANY),
        ],
        out_specs=(pl.BlockSpec(memory_space=VMEM), pl.BlockSpec(memory_space=pl.ANY)),
        scratch_shapes=[
            VMEM((N_T, 8, rows), jnp.float32),
            DMA((N_T - 1,)),
            DMA((N_T - 1,)),
            DMA((N_T - 1,)),
            DMA((N_T - 1,)),
            DMA,
        ],
        compiler_params=pltpu.CompilerParams(
            collective_id=1, has_side_effects=True, vmem_limit_bytes=32 * 2**20
        ),
        cost_estimate=pl.CostEstimate(flops=10**7, bytes_accessed=10**7, transcendentals=0),
    )(tokens, gain.reshape(N_T, 1, width), out_weight)


class Gather:
    def __init__(self, own_ref, buf, send_sem, recv_sem):
        me = lax.axis_index("tensor")
        y = lax.rem(me, 4)
        base = me - y
        self.me = me
        self.own_ref, self.buf, self.send_sem, self.recv_sem = own_ref, buf, send_sem, recv_sem
        self.up = base + lax.rem(y + 1, 4)
        self.down = base + lax.rem(y + 3, 4)
        far = base + lax.rem(y + 2, 4)

        def across(t):
            return lax.rem(t + 4, N_T)

        self.pair = across(me)
        self.owner = [
            self.down,
            self.up,
            self.pair,
            far,
            across(self.down),
            across(self.up),
            across(far),
        ]
        self.step = own_ref.shape[0] // SUBS
        self.started = []

    def greet(self):
        greet([self.up, self.down, self.pair])

    def greeted(self):
        greeted(3)

    def rows(self, s):
        return pl.ds(s * self.step, self.step)

    def send(self, src, owner, kind, s, to):
        copy = remote(
            src.at[self.rows(s)],
            self.buf.at[owner, self.rows(s)],
            self.send_sem.at[len(self.started)],
            self.recv_sem.at[kind, s],
            to,
        )
        copy.start()
        self.started.append(copy)

    def forward(self, owner, kind, s, to):
        self.send(self.buf.at[owner], owner, kind, s, to)

    def wait(self, kind, s):
        owner = self.owner[kind]
        place = self.buf.at[owner, self.rows(s)]
        remote(place, place, self.send_sem.at[0], self.recv_sem.at[kind, s], self.pair).wait_recv()

    def send_own(self):
        for s in range(SUBS):
            self.send(self.own_ref, self.me, 2, s, self.pair)
            self.send(self.own_ref, self.me, 0, s, self.up)
            self.send(self.own_ref, self.me, 1, s, self.down)

    def run(self, use):
        half = SUBS // 2
        self.send_own()
        use(self.own_ref, self.me)
        for s in range(SUBS):
            self.wait(0, s)
            if s < half:
                self.forward(self.owner[0], 3, s, self.up)
            self.wait(1, s)
            if s >= half:
                self.forward(self.owner[1], 3, s, self.down)
            self.wait(2, s)
            self.forward(self.pair, 4, s, self.up)
            self.forward(self.pair, 5, s, self.down)
        for kind in range(3):
            use(self.buf.at[self.owner[kind]], self.owner[kind])
        for s in range(SUBS):
            self.wait(4, s)
            if s < half:
                self.forward(self.owner[4], 6, s, self.up)
            self.wait(5, s)
            if s >= half:
                self.forward(self.owner[5], 6, s, self.down)
        for s in range(SUBS):
            self.wait(3, s)
        for kind in (3, 4, 5):
            use(self.buf.at[self.owner[kind]], self.owner[kind])
        for s in range(SUBS):
            self.wait(6, s)
        use(self.buf.at[self.owner[6]], self.owner[6])
        for copy in self.started:
            copy.wait_send()


GATHER_SENDS = 7 * SUBS
GATHER_SEMS = [DMA((GATHER_SENDS,)), DMA((7, SUBS))]


def project_kernel(own_ref, w_ref, bias_ref, out_ref, buf, w_buf, total, send_sem, recv_sem, w_sem):
    width = own_ref.shape[1]
    gather = Gather(own_ref, buf, send_sem, recv_sem)
    gather.greet()
    order = [gather.me] + gather.owner
    loads = []
    for i, t in enumerate(order):
        load = pltpu.make_async_copy(
            w_ref.at[pl.ds(pl.multiple_of(t * width, width), width)], w_buf.at[i], w_sem.at[i]
        )
        load.start()
        loads.append(load)
    gather.greeted()
    used = []

    def use(chunk, owner):
        i = len(used)
        used.append(owner)
        loads[i].wait()
        tile = min(256, total.shape[1])

        def one(n, _):
            cut = pl.ds(pl.multiple_of(n * tile, tile), tile)
            term = jnp.dot(chunk[...], w_buf[i, :, cut], preferred_element_type=jnp.float32)
            if i == 0:
                total[:, cut] = term
            else:
                total[:, cut] += term
            return 0

        lax.fori_loop(0, total.shape[1] // tile, one, 0)

    gather.run(use)
    bias = bias_ref[...].astype(jnp.float32)
    out_ref[...] = (total[...] + bias).astype(jnp.bfloat16)


def project(normed, weight, bias):
    rows, width = normed.shape
    columns = weight.shape[1]
    return pl.pallas_call(
        project_kernel,
        out_shape=jax.ShapeDtypeStruct((rows, columns), jnp.bfloat16),
        in_specs=[
            pl.BlockSpec(memory_space=VMEM),
            pl.BlockSpec(memory_space=pl.ANY),
            pl.BlockSpec(memory_space=VMEM),
        ],
        out_specs=pl.BlockSpec(memory_space=VMEM),
        scratch_shapes=[
            VMEM((N_T, rows, width), jnp.bfloat16),
            VMEM((N_T, width, columns), jnp.bfloat16),
            VMEM((rows, columns), jnp.float32),
            *GATHER_SEMS,
            DMA((N_T,)),
        ],
        compiler_params=pltpu.CompilerParams(
            collective_id=2, has_side_effects=True, vmem_limit_bytes=48 * 2**20
        ),
        cost_estimate=pl.CostEstimate(
            flops=2 * rows * width * N_T * columns,
            bytes_accessed=10**8,
            transcendentals=0,
        ),
    )(normed, weight, bias)


def output_kernel(
    own_ref, w_ref, out_ref, buf, w_buf, total, done, send_sem, recv_sem, w_sem, out_send, out_recv, own_sem
):
    me = lax.axis_index("tensor")
    gather = Gather(own_ref, buf, send_sem, recv_sem)
    others = all_others(me)
    greet(others)
    order = [gather.me] + gather.owner
    loads = []
    for i, t in enumerate(order):
        load = pltpu.make_async_copy(w_ref.at[:, t], w_buf.at[i], w_sem.at[i])
        load.start()
        loads.append(load)
    greeted(N_T - 1)
    used = []
    depth = own_ref.shape[1]
    columns = total.shape[1]

    def use(chunk, owner):
        i = len(used)
        used.append(owner)
        loads[i].wait()
        tile = min(256, columns)

        def one(n, _):
            cut = pl.ds(pl.multiple_of(n * tile, tile), tile)
            weight = w_buf[i, :, :, cut].reshape(depth, tile)
            term = jnp.dot(chunk[...], weight, preferred_element_type=jnp.float32)
            term = term.astype(jnp.bfloat16).astype(jnp.float32)
            if i == 0:
                total[:, cut] = term
            else:
                total[:, cut] += term
            return 0

        lax.fori_loop(0, columns // tile, one, 0)

    gather.run(use)
    done[...] = total[...].astype(jnp.bfloat16)
    part = out_ref.shape[0]

    def rows_of(t):
        return pl.ds(pl.multiple_of(t * part, part), part)

    place = out_ref.at[:, pl.ds(pl.multiple_of(me * columns, columns), columns)]
    copies = []
    for d, other in enumerate(others):
        copy = remote(done.at[rows_of(other)], place, out_send.at[d], out_recv.at[d], other)
        copy.start()
        copies.append(copy)
    own = pltpu.make_async_copy(done.at[rows_of(me)], place, own_sem)
    own.start()
    own.wait()
    for copy in copies:
        copy.wait()


def project_out(attended, weight):
    rows, depth = attended.shape
    columns = weight.shape[3]
    return pl.pallas_call(
        output_kernel,
        out_shape=jax.ShapeDtypeStruct((rows // N_T, columns * N_T), jnp.bfloat16),
        in_specs=[pl.BlockSpec(memory_space=VMEM), pl.BlockSpec(memory_space=pl.ANY)],
        out_specs=pl.BlockSpec(memory_space=pl.ANY),
        scratch_shapes=[
            VMEM((N_T, rows, depth), jnp.bfloat16),
            VMEM((N_T, weight.shape[0], weight.shape[2], columns), jnp.bfloat16),
            VMEM((rows, columns), jnp.float32),
            VMEM((rows, columns), jnp.bfloat16),
            *GATHER_SEMS,
            DMA((N_T,)),
            DMA((N_T - 1,)),
            DMA((N_T - 1,)),
            DMA,
        ],
        compiler_params=pltpu.CompilerParams(
            collective_id=3, has_side_effects=True, vmem_limit_bytes=48 * 2**20
        ),
        cost_estimate=pl.CostEstimate(
            flops=2 * rows * depth * N_T * columns, bytes_accessed=10**8, transcendentals=0
        ),
    )(attended, weight)


TILE_Q = 256
TILE_K = 256
LOW = -1e30


def attend_kernel(first_ref, start_ref, q_ref, k_ref, v_ref, out_ref):
    rows = q_ref.shape[0]
    heads = q_ref.shape[1] // HD
    factor = HD**-0.5 * 1.4426950408889634
    for a in range(rows // TILE_Q):
        base = first_ref[0] + a * TILE_Q
        start = start_ref[:, a * TILE_Q : (a + 1) * TILE_Q]
        query_row = base + lax.broadcasted_iota(jnp.int32, (1, TILE_Q), 1)
        low_tile = lax.div(first_ref[1 + a], TILE_K)
        high_tile = lax.div(base + TILE_Q, TILE_K)

        def one(i, carry, a=a, start=start, query_row=query_row, high_tile=high_tile):
            tile = high_tile - 1 - i
            cut = pl.ds(pl.multiple_of(tile * TILE_K, TILE_K), TILE_K)
            keys = k_ref[cut]
            values = v_ref[cut].T
            key_row = tile * TILE_K + lax.broadcasted_iota(jnp.int32, (TILE_K, TILE_Q), 0)
            allowed = (key_row >= start) & (key_row <= query_row)
            after = []
            for h in range(heads):
                top, denominator, weighted = carry[h]
                query = q_ref[a * TILE_Q : (a + 1) * TILE_Q, h * HD : (h + 1) * HD]
                scores = lax.dot_general(
                    keys, query, (((1,), (1,)), ((), ())), preferred_element_type=jnp.float32
                )
                scores = jnp.where(allowed, scores * factor, 2 * LOW)
                new_top = jnp.maximum(top, jnp.max(scores, axis=0, keepdims=True))
                weights = jnp.exp2(scores - new_top)
                shrink = jnp.exp2(top - new_top)
                denominator = denominator * shrink + jnp.sum(weights, axis=0, keepdims=True)
                coarse = weights.astype(jnp.bfloat16)
                fine = (weights - coarse.astype(jnp.float32)).astype(jnp.bfloat16)
                weighted = weighted * shrink
                weighted += jnp.dot(values, coarse, preferred_element_type=jnp.float32)
                weighted += jnp.dot(values, fine, preferred_element_type=jnp.float32)
                after.append((new_top, denominator, weighted))
            return tuple(after)

        begin = (
            jnp.full((1, TILE_Q), LOW, jnp.float32),
            jnp.zeros((1, TILE_Q), jnp.float32),
            jnp.zeros((HD, TILE_Q), jnp.float32),
        )
        ended = lax.fori_loop(0, high_tile - low_tile, one, (begin,) * heads)
        for h in range(heads):
            _, denominator, weighted = ended[h]
            out_ref[a * TILE_Q : (a + 1) * TILE_Q, h * HD : (h + 1) * HD] = (
                (weighted / denominator).T.astype(jnp.bfloat16)
            )


def attend(first_row, start, queries, keys, values):
    rows = queries.shape[0]
    scalars = jnp.concatenate([first_row[None], start[:: TILE_Q]]).astype(jnp.int32)
    vmem = pl.BlockSpec(memory_space=VMEM)
    return pl.pallas_call(
        attend_kernel,
        out_shape=jax.ShapeDtypeStruct(queries.shape, jnp.bfloat16),
        in_specs=[pl.BlockSpec(memory_space=pltpu.SMEM), vmem, vmem, vmem, vmem],
        out_specs=vmem,
        compiler_params=pltpu.CompilerParams(vmem_limit_bytes=40 * 2**20),
        cost_estimate=pl.CostEstimate(flops=10**9, bytes_accessed=10**7, transcendentals=10**7),
    )(scalars, start.reshape(1, rows), queries, keys, values)


def angle_tables(positions):
    half_size = HD // 2
    freqs = 1000000.0 ** (-(jnp.arange(half_size, dtype=jnp.float32) * 2.0) / HD)
    angles = positions.astype(jnp.float32)[:, None] * freqs[None, :]
    return (jnp.cos(angles), jnp.sin(angles))


def rotate_pairs(values, cosine, sine_part):
    half_size = HD // 2
    first_half = values[..., :half_size]
    second_half = values[..., half_size:]
    return jnp.concatenate(
        [
            first_half * cosine - second_half * sine_part,
            second_half * cosine + first_half * sine_part,
        ],
        axis=-1,
    )


def document_places(source_row, segment_id, rows):
    both = lax.all_gather(jnp.stack([source_row, segment_id]), ("dp", "ctx"), axis=0)
    sources = both[:, 0].reshape(-1)
    segments = both[:, 1].reshape(-1)
    count = sources.shape[0]
    of_doc = segments[None, :] == jnp.arange(DOC_IDS, dtype=jnp.int32)[:, None]
    rollout_start = jnp.min(jnp.where(of_doc, sources[None, :], count), axis=1)
    packed_start = jnp.min(
        jnp.where(of_doc, jnp.arange(count, dtype=jnp.int32)[None, :], count), axis=1
    )
    begun = rollout_start[None, :] <= rows[:, None]
    start = jnp.max(jnp.where(begun, rollout_start[None, :], 0), axis=1)
    shift = jnp.sum(
        jnp.where(
            begun & (rollout_start[None, :] == start[:, None]),
            (packed_start - rollout_start)[None, :],
            0,
        ),
        axis=1,
    )
    return start, rows + shift


def per_device(
    tokens, norm_gain, project_weight, project_bias, output_weight, source_row, segment_id
):
    local_rows = tokens.shape[0]
    replicas = lax.axis_size("dp") * lax.axis_size("ctx")
    first_row = lax.axis_index(("dp", "ctx")) * local_rows
    rows = first_row + jnp.arange(local_rows, dtype=jnp.int32)
    normed, shuffled = normalise(tokens, norm_gain, output_weight, replicas)
    out_columns = lax.all_gather(shuffled, ("dp", "ctx"), axis=0)
    start, place = document_places(source_row, segment_id, rows)
    projected = project(normed, project_weight.reshape(project_weight.shape[0], -1), project_bias)
    cosine, sine_part = angle_tables(lax.rem(place, PACK))
    stacked = projected.reshape(local_rows, GROUP + 2, HD)
    turned = rotate_pairs(
        stacked[:, : GROUP + 1].astype(jnp.float32), cosine[:, None], sine_part[:, None]
    ).astype(jnp.bfloat16)
    queries = turned[:, :GROUP].reshape(local_rows, GROUP * HD)
    own = jnp.concatenate([turned[:, GROUP], stacked[:, GROUP + 1]], axis=1)
    both = lax.all_gather(own, ("dp", "ctx"), axis=0, tiled=True)
    attended = attend(first_row, start, queries, both[:, :HD], both[:, HD:])
    return project_out(attended, out_columns)


def solution(mesh):
    placed = (
        P(("dp", "ctx"), "tensor"),
        P(),
        P(None, "tensor", None),
        P("tensor", None),
        P("tensor", None),
        P(("dp", "ctx")),
        P(("dp", "ctx")),
    )
    return jax.shard_map(
        per_device,
        mesh=mesh,
        in_specs=placed,
        out_specs=P(("dp", "ctx", "tensor"), None),
        check_vma=False,
    )
```

time: 561 us -> 280 us (0.50)
  waiting for transfers between devices: 360 us -> 79.8 us
  Pallas kernels: 0 us -> 152 us
  matrix products: 67 us -> 0 us
  local copies, waits for them, and re-layouts: 61 us -> 10.5 us
  other arithmetic: 27.3 us -> 3.34 us
  blocking collectives: 29.2 us -> 19.3 us
    all_gather x5 -> x2, waiting for transfers between devices: 245 us -> 79.1 us  [the longest x1 46.3 us: per_device(): out_columns = lax.all_gather(shuffled, ('dp', 'ctx'), axis=0)]
    pallas_call x0 -> x4, Pallas kernels: none -> 152 us  [the longest x1 74.7 us: project(): pl.pallas_call(project_kernel, out_shape=jax.ShapeDtypeStruct((rows, colu...]
    reduce_scatter x1 -> x0, waiting for transfers between devices: 115 us -> none  [per_device(): lax.psum_scatter(jnp.dot(unpacked, output_weight, preferred_element_type=...]
    dot_general x4 -> x0, matrix products: 67 us -> none  [the longest x1 28.7 us: per_device(): jnp.einsum('hqk,khd->hqd', weights, value_piece.astype(jnp.float32), prec...]
    scatter x1 -> x0, local copies, waits for them, and re-layouts: 35.9 us -> none  [per_device(): unpacked = jnp.zeros_like(attended).at[within].set(value_rows, mode='drop')]
    reduce_sum x2 -> x1, other arithmetic: 22 us -> 0.09 us  [document_places(): jnp.sum(jnp.where(begun & (rollout_start[None, :] == start[:, None]), (pa...]
    all_gather x1 -> x0, local copies, waits for them, and re-layouts: 11.9 us -> none  [per_device(): value_rows = lax.all_gather(attended, ('dp', 'ctx'), axis=0, tiled=True)]
    gather x1 -> x0, local copies, waits for them, and re-layouts: 10.7 us -> none  [per_device(): taken = jnp.take(shard_piece, jnp.clip(within, 0, length - 1), axis=0)]
  transfers between devices with their start and end apart: 6 -> 2, of which waited for: 5 -> 2; matrix products, arithmetic and copies ran while one was open for 6% -> 1% of each run, Pallas kernels for 0% -> 2%
where the time goes in v1:
time: 280 us; the launch traced here: 278 us
  Pallas kernels  152 us (54%)
  waiting for transfers between devices  79.8 us (28%)
  blocking collectives  19.3 us (7%)
  between operations  13.6 us (5%)
  local copies, waits for them, and re-layouts  10.5 us (4%)
  other arithmetic  3.34 us (1%)
    pallas_call x1, Pallas kernels, project(): pl.pallas_call(project_kernel, out_shape=jax.ShapeDtypeStruct((rows, colu...  74.7 us
    pallas_call x1, Pallas kernels, project_out(): pl.pallas_call(output_kernel, out_shape=jax.ShapeDtypeStruct((rows // N_T...  57 us
    all_gather x1, waiting for transfers between devices, per_device(): out_columns = lax.all_gather(shuffled, ('dp', 'ctx'), axis=0)  46.3 us
    all_gather x1, waiting for transfers between devices, per_device(): both = lax.all_gather(own, ('dp', 'ctx'), axis=0, tiled=True)  32.8 us
    all_gather x1, blocking collectives, document_places(): lax.all_gather(jnp.stack([source_row, segment_id]), ('dp', 'ctx'), axis=0)  19.3 us
    pallas_call x1, Pallas kernels, normalise(): pl.pallas_call(functools.partial(norm_kernel, width * N_T), out_shape=(ja...  14.7 us
    unnamed x15, local copies, waits for them, and re-layouts  7.08 us
  transfers between devices with their start and end apart: 2, of which 2 were waited for; matrix products, arithmetic and copies ran while one was open for 1% of the time, Pallas kernels for 2%

profile of v1, /device:TPU:32, one launch (start us, length us, event | category | flops | bytes accessed | tf_op | source)
XLA Modules:
  0.0 278.1 jit_solution(12089615097188562341)
XLA Ops:
  6.6 3.4 %copy-done = bf16[512,8192]{1,0:T(8,128)(2,1)S(1)} copy-done((bf16[512,8192]{1,0:T(8,128)(2,1)S(1)}, bf16[512,8192]{1,0:T(8,128)(2,1)}, u32[]{:S(2)}) %copy-start) | copy-done | bytes 8388632
  9.9 1.2 copy-done.1
  11.2 0.8 copy-done.2
  11.9 14.7 %shard_map.73 = (bf16[512,1024]{1,0:T(8,128)(2,1)S(1)}, bf16[8,32,1024]{2,1,0:T(8,128)(2,1)}) custom-call(bf16[512,1024]{1,0:T(8,128)(2,1)S(1)} %copy-done.1, f32[8,1,1024]{2,1,0:T(1,128)S(1)} %bitcast.16, bf16[512,8192]{1,0:T(8,128)(2,1)S(1)} %copy-done), custom_call_target="tpu_custom_call" | custom-call | flops 10000000 | bytes 10000000 | tf_op jit(solution)/shard_map/pallas_call | solution.py:127
  26.6 74.7 %shard_map.74 = bf16[512,768]{1,0:T(8,128)(2,1)S(1)} custom-call(bf16[512,1024]{1,0:T(8,128)(2,1)S(1)} %get-tuple-element.7.own_ref, bf16[8192,768]{1,0:T(8,128)(2,1)} %bitcast.26, bf16[1,768]{1,0:T(2,128)(2,1)S(1)} %copy-done.3), custom_call_target="tpu_custom_call" | custom-call | flops 6442450944 | bytes 100000000 | tf_op jit(solution)/shard_map/pallas_call | solution.py:293
  101.3 0.3 copy.18
  101.7 0.3 copy-done.4
  102.0 19.3 %all-gather.2 = s32[16,2,512]{2,1,0:T(2,128)S(1)} all-gather(s32[1,2,512]{2,1,0:T(2,128)S(1)} %add_bitcast_fusion), channel_id=2, replica_groups=mesh['dp'=2,'ctx'=8,'tensor'=8] {'dp','ctx'}, dimensions={0}, use_global_device_ids=true | all-gather | bytes 69632 | tf_op jit(solution)/shard_map/all_gather | solution.py:496
  121.3 0.3 copy.23
  121.8 0.3 select_reduce_fusion
  122.3 0.1 copy.24
  122.4 1.0 multiply_cosine_fusion
  123.4 0.5 add_convert_fusion
  124.0 0.7 pad_maximum_fusion
  124.8 0.7 all-gather.8.cloned.1.call-update
  125.6 0.3 fusion
  125.9 0.2 copy.20
  126.2 0.2 copy.22.q_ref
  126.5 32.8 %all-gather.6.cloned.1.call-done = bf16[8192,256]{1,0:T(8,128)(2,1)} async-done(((bf16[512,256]{1,0:T(8,128)(2,1)}), bf16[8192,256]{1,0:T(8,128)(2,1)}) %all-gather.6.cloned.1.call-update) | async-done | bytes 4194320 | tf_op jit(solution)/shard_map/all_gather | solution.py:536
  159.3 2.5 fusion.5
  161.7 5.3 %shard_map.75.own_ref = bf16[512,512]{1,0:T(8,128)(2,1)S(1)} custom-call(s32[3]{0:T(128)S(1)} %pad_add_fusion.first_ref, s32[1,512]{1,0:T(1,128)S(1)} %bitcast.17, bf16[512,512]{1,0:T(8,128)(2,1)S(1)} %copy.22.q_ref, bf16[8192,128]{1,0:T(8,128)(2,1)S(1)} %get-tuple-element.12.k_ref, bf16[8192,128]{1,0:T(8,128)(2,1)S(1)} %get-tuple-element.11.v_ref), custom_call_target="tpu_custom_call" | custom-call | flops 1000000000 | bytes 10000000 | tf_op jit(solution)/shard_map/pallas_call | solution.py:465
  167.0 46.3 %all-gather.8.cloned.1.call-done = bf16[128,32,1024]{2,1,0:T(8,128)(2,1)} async-done(((bf16[8,32,1024]{2,1,0:T(8,128)(2,1)}), bf16[128,32,1024]{2,1,0:T(8,128)(2,1)}) %all-gather.8.cloned.1.call-update) | async-done | bytes 8388624 | tf_op jit(solution)/shard_map/all_gather | solution.py:526
  213.3 57.0 %shard_map.76 = bf16[64,8192]{1,0:T(8,128)(2,1)S(1)} custom-call(bf16[512,512]{1,0:T(8,128)(2,1)S(1)} %shard_map.75.own_ref, bf16[16,8,32,1024]{3,2,1,0:T(8,128)(2,1)} %bitcast.27), custom_call_target="tpu_custom_call" | custom-call | flops 4294967296 | bytes 100000000 | tf_op jit(solution)/shard_map/pallas_call | solution.py:380
  270.3 1.0 copy.26
  (25 shorter events, 0.8 us)
Async XLA Ops:
  6.5 152.7 %all-gather.6.cloned.1.call-start = ((), (), s32[]{:S(2)}) async-start(), calls=%async_computation | async-start | bytes 4456448 | tf_op jit(solution)/shard_map/all_gather | solution.py:536
  6.5 3.4 %copy-start = (bf16[512,8192]{1,0:T(8,128)(2,1)S(1)}, bf16[512,8192]{1,0:T(8,128)(2,1)}, u32[]{:S(2)}) copy-start(bf16[512,8192]{1,0:T(8,128)(2,1)} %wo_ref.1) | copy-start | bytes 25165828
  9.9 1.2 copy-start.1
  11.2 0.8 copy-start.2
  11.9 14.7 %copy-start.3 = (bf16[1,768]{1,0:T(2,128)(2,1)S(1)}, bf16[1,768]{1,0:T(2,128)(2,1)}, u32[]{:S(2)}) copy-start(bf16[1,768]{1,0:T(2,128)(2,1)} %bias_ref.1) | copy-start | bytes 4612
  101.3 0.7 copy-start.4
  101.3 0.7 copy-start.5
  124.8 88.5 %all-gather.8.cloned.1.call-start = ((), (), s32[]{:S(2)}) async-start(), calls=%async_computation.1 | async-start | bytes 8912896 | tf_op jit(solution)/shard_map/all_gather | solution.py:526
Sparse Core Ops, SparseCore 0:
  124.9 34.2 all-gather.5
  161.0 52.2 all-gather.7

commit v2 on v1

--- a/solution.py
+++ b/solution.py
@@ -52,21 +52,46 @@
     tok_ref,
     gain_ref,
     wo_ref,
+    places_ref,
     normed_ref,
     shuffled_ref,
+    spots_ref,
     stats,
+    docs,
     stat_send,
     stat_recv,
     w_send,
     w_recv,
+    doc_send,
+    doc_recv,
     own_sem,
 ):
     me = lax.axis_index("tensor")
     replica = lax.axis_index("dp") * lax.axis_size("ctx") + lax.axis_index("ctx")
+    replicas = docs.shape[0]
     rows, width = tok_ref.shape
     piece, columns = shuffled_ref.shape[1:]
     others = all_others(me)
     greet(others)
+    alike = [ring_of(lax.rem(replica + d, replicas)) for d in range(1, replicas)]
+    for other in alike:
+        pl.semaphore_signal(
+            pltpu.get_barrier_semaphore(), inc=1, device_id=other, device_id_type=MESH
+        )
+    sources = places_ref[0:1]
+    segments = places_ref[1:2]
+    packed_row = replica * rows + lax.broadcasted_iota(jnp.int32, (1, rows), 1)
+    none = rows * replicas
+    lane = lax.broadcasted_iota(jnp.int32, (8, 128), 1)
+    line = lax.broadcasted_iota(jnp.int32, (8, 128), 0)
+    table = jnp.full((8, 128), none, jnp.int32)
+    for doc in range(DOC_IDS):
+        of_doc = segments == doc
+        first_source = jnp.min(jnp.where(of_doc, sources, none), axis=1, keepdims=True)
+        first_packed = jnp.min(jnp.where(of_doc, packed_row, none), axis=1, keepdims=True)
+        found = jnp.where(line == 0, first_source, first_packed)
+        table = jnp.where(lane == doc, found, table)
+    docs[pl.ds(replica, 1)] = table[None]
     block = 128
     for i in range(rows // block):
         total = jnp.zeros((block, 128), jnp.float32)
@@ -77,7 +102,7 @@
         stats[pl.ds(me, 1), :, i * block : (i + 1) * block] = jnp.broadcast_to(
             summed[None], (1, 8, block)
         )
-    greeted(N_T - 1)
+    greeted(N_T - 1 + replicas - 1)
     mine = pl.ds(pl.multiple_of(replica * piece, piece), piece)
 
     def columns_of(index):
@@ -91,6 +116,18 @@
         )
         copy.start()
         stat_copies.append(copy)
+    doc_copies = []
+    for d, other in enumerate(alike):
+        copy = pltpu.make_async_remote_copy(
+            src_ref=docs.at[replica],
+            dst_ref=docs.at[replica],
+            send_sem=doc_send.at[d],
+            recv_sem=doc_recv.at[d],
+            device_id=other,
+            device_id_type=MESH,
+        )
+        copy.start()
+        doc_copies.append(copy)
     for d, other in enumerate(others):
         copy = remote(
             wo_ref.at[mine, columns_of(other)],
@@ -115,12 +152,34 @@
             cut = (slice(i * block, (i + 1) * block), slice(j * 128, (j + 1) * 128))
             gain = gain_ref[me, :, j * 128 : (j + 1) * 128]
             normed_ref[cut] = (tok_ref[cut].astype(jnp.float32) * along * gain).astype(jnp.bfloat16)
+    for copy in doc_copies:
+        copy.wait()
+    table = docs[0]
+    for r in range(1, replicas):
+        table = jnp.minimum(table, docs[r])
+    row = replica * rows + lax.broadcasted_iota(jnp.int32, (1, rows), 1)
+    start = jnp.full((1, rows), -1, jnp.int32)
+    place = row
+    for doc in range(DOC_IDS):
+        first_source = table[0:1, doc : doc + 1]
+        first_packed = table[1:2, doc : doc + 1]
+        later = (first_source <= row) & (first_source > start)
+        start = jnp.where(later, first_source, start)
+        place = jnp.where(later, row + (first_packed - first_source), place)
+    spots_ref[...] = jnp.where(
+        lax.broadcasted_iota(jnp.int32, (8, rows), 0) == 0, start, place
+    )
     own.wait()
     for copy in w_copies:
         copy.wait()
 
 
-def normalise(tokens, gain, out_weight, replicas):
+def ring_of(replica):
+    per = lax.axis_size("ctx")
+    return {"dp": lax.div(replica, per), "ctx": lax.rem(replica, per)}
+
+
+def normalise(tokens, gain, out_weight, places, replicas):
     rows, width = tokens.shape
     depth, out_width = out_weight.shape
     piece, columns = depth // replicas, out_width // N_T
@@ -129,26 +188,35 @@
         out_shape=(
             jax.ShapeDtypeStruct((rows, width), jnp.bfloat16),
             jax.ShapeDtypeStruct((N_T, piece, columns), jnp.bfloat16),
+            jax.ShapeDtypeStruct((8, rows), jnp.int32),
         ),
         in_specs=[
             pl.BlockSpec(memory_space=VMEM),
             pl.BlockSpec(memory_space=VMEM),
-            pl.BlockSpec(memory_space=pl.ANY),
+            pl.BlockSpec(memory_space=pltpu.HBM),
+            pl.BlockSpec(memory_space=VMEM),
         ],
-        out_specs=(pl.BlockSpec(memory_space=VMEM), pl.BlockSpec(memory_space=pl.ANY)),
+        out_specs=(
+            pl.BlockSpec(memory_space=VMEM),
+            pl.BlockSpec(memory_space=pltpu.HBM),
+            pl.BlockSpec(memory_space=VMEM),
+        ),
         scratch_shapes=[
             VMEM((N_T, 8, rows), jnp.float32),
+            VMEM((replicas, 8, 128), jnp.int32),
             DMA((N_T - 1,)),
             DMA((N_T - 1,)),
             DMA((N_T - 1,)),
             DMA((N_T - 1,)),
+            DMA((replicas - 1,)),
+            DMA((replicas - 1,)),
             DMA,
         ],
         compiler_params=pltpu.CompilerParams(
-            collective_id=1, has_side_effects=True, vmem_limit_bytes=32 * 2**20
+            collective_id=1, has_side_effects=True, vmem_limit_bytes=58 * 2**20
         ),
         cost_estimate=pl.CostEstimate(flops=10**7, bytes_accessed=10**7, transcendentals=0),
-    )(tokens, gain.reshape(N_T, 1, width), out_weight)
+    )(tokens, gain.reshape(N_T, 1, width), out_weight, places)
 
 
 class Gather:
@@ -295,7 +363,7 @@
         out_shape=jax.ShapeDtypeStruct((rows, columns), jnp.bfloat16),
         in_specs=[
             pl.BlockSpec(memory_space=VMEM),
-            pl.BlockSpec(memory_space=pl.ANY),
+            pl.BlockSpec(memory_space=pltpu.HBM),
             pl.BlockSpec(memory_space=VMEM),
         ],
         out_specs=pl.BlockSpec(memory_space=VMEM),
@@ -380,8 +448,8 @@
     return pl.pallas_call(
         output_kernel,
         out_shape=jax.ShapeDtypeStruct((rows // N_T, columns * N_T), jnp.bfloat16),
-        in_specs=[pl.BlockSpec(memory_space=VMEM), pl.BlockSpec(memory_space=pl.ANY)],
-        out_specs=pl.BlockSpec(memory_space=pl.ANY),
+        in_specs=[pl.BlockSpec(memory_space=VMEM), pl.BlockSpec(memory_space=pltpu.HBM)],
+        out_specs=pl.BlockSpec(memory_space=pltpu.HBM),
         scratch_shapes=[
             VMEM((N_T, rows, depth), jnp.bfloat16),
             VMEM((N_T, weight.shape[0], weight.shape[2], columns), jnp.bfloat16),
@@ -407,7 +475,7 @@
 LOW = -1e30
 
 
-def attend_kernel(first_ref, start_ref, q_ref, k_ref, v_ref, out_ref):
+def attend_kernel(first_ref, start_ref, q_ref, kv_ref, out_ref):
     rows = q_ref.shape[0]
     heads = q_ref.shape[1] // HD
     factor = HD**-0.5 * 1.4426950408889634
@@ -421,8 +489,8 @@
         def one(i, carry, a=a, start=start, query_row=query_row, high_tile=high_tile):
             tile = high_tile - 1 - i
             cut = pl.ds(pl.multiple_of(tile * TILE_K, TILE_K), TILE_K)
-            keys = k_ref[cut]
-            values = v_ref[cut].T
+            keys = kv_ref[cut, :HD]
+            values = kv_ref[cut, HD:].T
             key_row = tile * TILE_K + lax.broadcasted_iota(jnp.int32, (TILE_K, TILE_Q), 0)
             allowed = (key_row >= start) & (key_row <= query_row)
             after = []
@@ -458,18 +526,18 @@
             )
 
 
-def attend(first_row, start, queries, keys, values):
+def attend(first_row, start, queries, both):
     rows = queries.shape[0]
     scalars = jnp.concatenate([first_row[None], start[:: TILE_Q]]).astype(jnp.int32)
     vmem = pl.BlockSpec(memory_space=VMEM)
     return pl.pallas_call(
         attend_kernel,
         out_shape=jax.ShapeDtypeStruct(queries.shape, jnp.bfloat16),
-        in_specs=[pl.BlockSpec(memory_space=pltpu.SMEM), vmem, vmem, vmem, vmem],
+        in_specs=[pl.BlockSpec(memory_space=pltpu.SMEM), vmem, vmem, vmem],
         out_specs=vmem,
         compiler_params=pltpu.CompilerParams(vmem_limit_bytes=40 * 2**20),
         cost_estimate=pl.CostEstimate(flops=10**9, bytes_accessed=10**7, transcendentals=10**7),
-    )(scalars, start.reshape(1, rows), queries, keys, values)
+    )(scalars, start.reshape(1, rows), queries, both)
 
 
 def angle_tables(positions):
@@ -479,40 +547,142 @@
     return (jnp.cos(angles), jnp.sin(angles))
 
 
-def rotate_pairs(values, cosine, sine_part):
-    half_size = HD // 2
-    first_half = values[..., :half_size]
-    second_half = values[..., half_size:]
-    return jnp.concatenate(
-        [
-            first_half * cosine - second_half * sine_part,
-            second_half * cosine + first_half * sine_part,
+SEEN_CHIPS = 4
+
+
+def turn_kernel(proj_ref, cos_ref, sin_ref, q_ref, kv_ref, own, own_sem, send_sem, recv_sem, near_send, near_recv):
+    per = lax.axis_size("ctx") // 2
+    ctx = lax.axis_index("ctx")
+    core = lax.rem(ctx, 2)
+    chip = lax.axis_index("dp") * per + lax.div(ctx, 2)
+    chips = lax.axis_size("dp") * per
+    block = chip * 2 + core
+    sibling = {"ctx": ctx + 1 - 2 * core}
+    rows = proj_ref.shape[0]
+
+    def same_core(other):
+        return {"dp": lax.div(other, per), "ctx": lax.rem(other, per) * 2 + core}
+
+    def signal(other):
+        pl.semaphore_signal(
+            pltpu.get_barrier_semaphore(), inc=1, device_id=other, device_id_type=MESH
+        )
+
+    signal(sibling)
+    for k in range(1, chips):
+        signal(same_core(lax.rem(chip + k, chips)))
+
+    cosine, sine = cos_ref[...], sin_ref[...]
+
+    def turned(slot):
+        wide = proj_ref[:, slot * HD : (slot + 1) * HD].astype(jnp.float32)
+        return (wide * cosine + pltpu.roll(wide, HD // 2, 1) * sine).astype(jnp.bfloat16)
+
+    own[:, :HD] = turned(GROUP)
+    own[:, HD:] = proj_ref[:, (GROUP + 1) * HD :]
+
+    greeted(chips)
+
+    def to_chip(k):
+        return pltpu.make_async_remote_copy(
+            src_ref=own,
+            dst_ref=kv_ref.at[block],
+            send_sem=send_sem.at[k - 1],
+            recv_sem=recv_sem.at[k - 1],
+            device_id=same_core(chip + k),
+            device_id_type=MESH,
+        )
+
+    def to_sibling(k):
+        place = kv_ref.at[block - 2 * k]
+        return pltpu.make_async_remote_copy(
+            src_ref=own if k == 0 else place,
+            dst_ref=place,
+            send_sem=near_send.at[k],
+            recv_sem=near_recv.at[k],
+            device_id=sibling,
+            device_id_type=MESH,
+        )
+
+    order = (2, 1, 3, 4)
+    for k in order:
+
+        @pl.when(chip + k < chips)
+        def _(k=k):
+            to_chip(k).start()
+
+    to_sibling(0).start()
+    keep = pltpu.make_async_copy(own, kv_ref.at[block], own_sem)
+    keep.start()
+    for head in range(GROUP):
+        q_ref[:, head * HD : (head + 1) * HD] = turned(head)
+    for k in (1, 3, 4, 2):
+
+        @pl.when(chip - k >= 0)
+        def _(k=k):
+            place = kv_ref.at[block - 2 * k]
+            pltpu.make_async_remote_copy(
+                src_ref=place,
+                dst_ref=place,
+                send_sem=send_sem.at[k - 1],
+                recv_sem=recv_sem.at[k - 1],
+                device_id=sibling,
+                device_id_type=MESH,
+            ).wait_recv()
+            to_sibling(k).start()
+
+    keep.wait()
+    sibling_block = block + 1 - 2 * core
+
+    def from_sibling(k):
+        place = kv_ref.at[sibling_block - 2 * k]
+        pltpu.make_async_remote_copy(
+            src_ref=place,
+            dst_ref=place,
+            send_sem=near_send.at[k],
+            recv_sem=near_recv.at[k],
+            device_id=sibling,
+            device_id_type=MESH,
+        ).wait_recv()
+
+    to_sibling(0).wait_send()
+    from_sibling(0)
+    for k in range(1, SEEN_CHIPS + 1):
+
+        @pl.when(chip - k >= 0)
+        def _(k=k):
+            to_sibling(k).wait_send()
+            from_sibling(k)
+
+        @pl.when(chip + k < chips)
+        def _(k=k):
+            to_chip(k).wait_send()
+
+
+def turn_and_share(projected, cosine, sine, replicas):
+    rows = projected.shape[0]
+    vmem = pl.BlockSpec(memory_space=VMEM)
+    return pl.pallas_call(
+        turn_kernel,
+        out_shape=(
+            jax.ShapeDtypeStruct((rows, GROUP * HD), jnp.bfloat16),
+            jax.ShapeDtypeStruct((replicas, rows, 2 * HD), jnp.bfloat16),
+        ),
+        in_specs=[vmem, vmem, vmem],
+        out_specs=(vmem, pl.BlockSpec(memory_space=pltpu.HBM)),
+        scratch_shapes=[
+            VMEM((rows, 2 * HD), jnp.bfloat16),
+            DMA,
+            DMA((SEEN_CHIPS,)),
+            DMA((SEEN_CHIPS,)),
+            DMA((SEEN_CHIPS + 1,)),
+            DMA((SEEN_CHIPS + 1,)),
         ],
-        axis=-1,
-    )
-
-
-def document_places(source_row, segment_id, rows):
-    both = lax.all_gather(jnp.stack([source_row, segment_id]), ("dp", "ctx"), axis=0)
-    sources = both[:, 0].reshape(-1)
-    segments = both[:, 1].reshape(-1)
-    count = sources.shape[0]
-    of_doc = segments[None, :] == jnp.arange(DOC_IDS, dtype=jnp.int32)[:, None]
-    rollout_start = jnp.min(jnp.where(of_doc, sources[None, :], count), axis=1)
-    packed_start = jnp.min(
-        jnp.where(of_doc, jnp.arange(count, dtype=jnp.int32)[None, :], count), axis=1
-    )
-    begun = rollout_start[None, :] <= rows[:, None]
-    start = jnp.max(jnp.where(begun, rollout_start[None, :], 0), axis=1)
-    shift = jnp.sum(
-        jnp.where(
-            begun & (rollout_start[None, :] == start[:, None]),
-            (packed_start - rollout_start)[None, :],
-            0,
-        ),
-        axis=1,
-    )
-    return start, rows + shift
+        compiler_params=pltpu.CompilerParams(
+            collective_id=4, has_side_effects=True, vmem_limit_bytes=24 * 2**20
+        ),
+        cost_estimate=pl.CostEstimate(flops=10**7, bytes_accessed=10**7, transcendentals=0),
+    )(projected, cosine, sine)
 
 
 def per_device(
@@ -521,20 +691,16 @@
     local_rows = tokens.shape[0]
     replicas = lax.axis_size("dp") * lax.axis_size("ctx")
     first_row = lax.axis_index(("dp", "ctx")) * local_rows
-    rows = first_row + jnp.arange(local_rows, dtype=jnp.int32)
-    normed, shuffled = normalise(tokens, norm_gain, output_weight, replicas)
+    places = jnp.stack([source_row, segment_id])
+    normed, shuffled, spots = normalise(tokens, norm_gain, output_weight, places, replicas)
     out_columns = lax.all_gather(shuffled, ("dp", "ctx"), axis=0)
-    start, place = document_places(source_row, segment_id, rows)
     projected = project(normed, project_weight.reshape(project_weight.shape[0], -1), project_bias)
-    cosine, sine_part = angle_tables(lax.rem(place, PACK))
-    stacked = projected.reshape(local_rows, GROUP + 2, HD)
-    turned = rotate_pairs(
-        stacked[:, : GROUP + 1].astype(jnp.float32), cosine[:, None], sine_part[:, None]
-    ).astype(jnp.bfloat16)
-    queries = turned[:, :GROUP].reshape(local_rows, GROUP * HD)
-    own = jnp.concatenate([turned[:, GROUP], stacked[:, GROUP + 1]], axis=1)
-    both = lax.all_gather(own, ("dp", "ctx"), axis=0, tiled=True)
-    attended = attend(first_row, start, queries, both[:, :HD], both[:, HD:])
+    start = spots[0]
+    cosine, sine = angle_tables(lax.rem(spots[1], PACK))
+    cosine = jnp.concatenate([cosine, cosine], axis=1)
+    sine = jnp.concatenate([-sine, sine], axis=1)
+    queries, both = turn_and_share(projected, cosine, sine, replicas)
+    attended = attend(first_row, start, queries, both.reshape(-1, 2 * HD))
     return project_out(attended, out_columns)
 
 

time: 280 us -> 200 us (0.71)
  waiting for transfers between devices: 79.8 us -> 0.04 us
  Pallas kernels: 152 us -> 178 us
  blocking collectives: 19.3 us -> 0 us
  local copies, waits for them, and re-layouts: 10.5 us -> 3.09 us
    all_gather x1, waiting for transfers between devices: 46.3 us -> 0.02 us  [per_device(): out_columns = lax.all_gather(shuffled, ('dp', 'ctx'), axis=0)]
    all_gather x1 -> x0, waiting for transfers between devices: 32.8 us -> none  [per_device(): both = lax.all_gather(own, ('dp', 'ctx'), axis=0, tiled=True)]
    pallas_call x0 -> x1, Pallas kernels: none -> 28 us  [turn_and_share(): pl.pallas_call(turn_kernel, out_shape=(jax.ShapeDtypeStruct((rows, GROUP...]
    all_gather x1 -> x0, blocking collectives: 19.3 us -> none  [document_places(): lax.all_gather(jnp.stack([source_row, segment_id]), ('dp', 'ctx'), axis=0)]
    pallas_call x1, Pallas kernels: 57 us -> 51.4 us  [project_out(): pl.pallas_call(output_kernel, out_shape=jax.ShapeDtypeStruct((rows // N_T...]
    unnamed x15 -> x5, local copies, waits for them, and re-layouts: 7.08 us -> 2.19 us
    pallas_call x1, Pallas kernels: 14.7 us -> 17.7 us  [normalise(): pl.pallas_call(functools.partial(norm_kernel, width * N_T), out_shape=(ja...]
  transfers between devices with their start and end apart: 2 -> 1, of which waited for: 2 -> 0; matrix products, arithmetic and copies ran while one was open for 1% -> 1% of each run, Pallas kernels for 2% -> 55%
where the time goes in v2:
time: 200 us; the launch traced here: 197 us
  Pallas kernels  178 us (89%)
  between operations  13.5 us (7%)
  local copies, waits for them, and re-layouts  3.09 us (2%)
  other arithmetic  2.61 us (1%)
    pallas_call x1, Pallas kernels, project(): pl.pallas_call(project_kernel, out_shape=jax.ShapeDtypeStruct((rows, colu...  74.1 us
    pallas_call x1, Pallas kernels, project_out(): pl.pallas_call(output_kernel, out_shape=jax.ShapeDtypeStruct((rows // N_T...  51.4 us
    pallas_call x1, Pallas kernels, turn_and_share(): pl.pallas_call(turn_kernel, out_shape=(jax.ShapeDtypeStruct((rows, GROUP...  28 us
    pallas_call x1, Pallas kernels, normalise(): pl.pallas_call(functools.partial(norm_kernel, width * N_T), out_shape=(ja...  17.7 us
    pallas_call x1, Pallas kernels, attend(): pl.pallas_call(attend_kernel, out_shape=jax.ShapeDtypeStruct(queries.shap...  6.68 us
  transfers between devices with their start and end apart: 1, of which 0 were waited for; matrix products, arithmetic and copies ran while one was open for 1% of the time, Pallas kernels for 55%

profile of v2, /device:TPU:32, one launch (start us, length us, event | category | flops | bytes accessed | tf_op | source)
XLA Modules:
  0.0 197.0 jit_solution(4910882983834812273)
XLA Ops:
  6.5 0.0 copy-start.1
  6.5 0.0 all-gather.3.cloned.1.call-start
  6.5 1.3 pad_add_fusion.places_ref
  7.8 17.7 %shard_map.73 = (bf16[512,1024]{1,0:T(8,128)(2,1)}, bf16[8,32,1024]{2,1,0:T(8,128)(2,1)}, s32[8,512]{1,0:T(8,128)}) custom-call(bf16[512,1024]{1,0:T(8,128)(2,1)} %tok_ref.1, f32[8,1,1024]{2,1,0:T(1,128)} %bitcast.11, bf16[512,8192]{1,0:T(8,128)(2,1)} %wo_ref.1, s32[2,512]{1,0:T(2,128)} %pad_add_fusion.places_ref), custom_call_target="tpu_custom_call" | custom-call | flops 10000000 | bytes 10000000 | tf_op jit(solution)/shard_map/pallas_call | solution.py:186
  25.6 0.0 all-gather.3.cloned.1.call-update
  25.6 0.8 fusion.3
  26.4 0.1 slice.10
  26.5 1.0 fusion
  27.5 0.2 pad_maximum_fusion
  27.7 0.0 copy-done.1
  27.7 0.0 copy-start
  27.7 1.2 copy-done
  29.0 74.1 %shard_map.74.proj_ref = bf16[512,768]{1,0:T(8,128)(2,1)S(1)} custom-call(bf16[512,1024]{1,0:T(8,128)(2,1)S(1)} %copy-done, bf16[8192,768]{1,0:T(8,128)(2,1)} %bitcast.15, bf16[1,768]{1,0:T(2,128)(2,1)S(1)} %copy-done.1), custom_call_target="tpu_custom_call" | custom-call | flops 6442450944 | bytes 100000000 | tf_op jit(solution)/shard_map/pallas_call | solution.py:361
  103.0 28.0 %shard_map.75 = (bf16[512,512]{1,0:T(8,128)(2,1)S(1)}, bf16[16,512,256]{2,1,0:T(8,128)(2,1)S(1)}) custom-call(bf16[512,768]{1,0:T(8,128)(2,1)S(1)} %shard_map.74.proj_ref, f32[512,128]{1,0:T(8,128)S(1)} %get-tuple-element.20.cos_ref, f32[512,128]{1,0:T(8,128)S(1)} %get-tuple-element.21.sin_ref), custom_call_target="tpu_custom_call" | custom-call | flops 10000000 | bytes 10000000 | tf_op jit(solution)/shard_map/pallas_call | solution.py:665
  131.0 0.1 pad_add_fusion.1.first_ref
  131.1 6.7 %shard_map.76.own_ref = bf16[512,512]{1,0:T(8,128)(2,1)S(1)} custom-call(s32[3]{0:T(128)S(1)} %pad_add_fusion.1.first_ref, s32[1,512]{1,0:T(1,128)S(1)} %get-tuple-element.16.start_ref, bf16[512,512]{1,0:T(8,128)(2,1)S(1)} %get-tuple-element.12.q_ref, bf16[8192,256]{1,0:T(8,128)(2,1)S(1)} %bitcast.10), custom_call_target="tpu_custom_call" | custom-call | flops 1000000000 | bytes 10000000 | tf_op jit(solution)/shard_map/pallas_call | solution.py:533
  137.8 0.0 all-gather.3.cloned.1.call-done
  137.8 51.4 %shard_map.77 = bf16[64,8192]{1,0:T(8,128)(2,1)S(1)} custom-call(bf16[512,512]{1,0:T(8,128)(2,1)S(1)} %shard_map.76.own_ref, bf16[16,8,32,1024]{3,2,1,0:T(8,128)(2,1)} %bitcast.16), custom_call_target="tpu_custom_call" | custom-call | flops 4294967296 | bytes 100000000 | tf_op jit(solution)/shard_map/pallas_call | solution.py:448
  189.2 1.0 copy.9
  (2 shorter events, 0.0 us)
Async XLA Ops:
  6.5 21.2 %copy-start.1 = (bf16[1,768]{1,0:T(2,128)(2,1)S(1)}, bf16[1,768]{1,0:T(2,128)(2,1)}, u32[]{:S(2)}) copy-start(bf16[1,768]{1,0:T(2,128)(2,1)} %bias_ref.1) | copy-start | bytes 4612
  6.5 131.3 %all-gather.3.cloned.1.call-start = ((), (), s32[]{:S(2)}) async-start(), calls=%async_computation | async-start | bytes 8912896 | tf_op jit(solution)/shard_map/all_gather | solution.py:696
  27.7 1.2 copy-start
Sparse Core Ops, SparseCore 0:
  25.7 71.3 all-gather.2

commit v3 on v0

v3 whole, which is shorter than its diff:
```python
import jax
import jax.numpy as jnp
import numpy as np
from jax import lax
from jax.experimental import pallas as pl
from jax.experimental.pallas import tpu as pltpu
from jax.sharding import PartitionSpec as P

HD = 128
GROUP = 4
PACK = 4096
DOC_IDS = 12
N_T = 8
SUBS = 4
DEPTH = 2
MESH = pl.DeviceIdType.MESH
VMEM = pltpu.VMEM
DMA = pltpu.SemaphoreType.DMA


def peer(index):
    return {"tensor": index}


def greet(others):
    barrier = pltpu.get_barrier_semaphore()
    for other in others:
        pl.semaphore_signal(barrier, inc=1, device_id=peer(other), device_id_type=MESH)


def greeted(count):
    pl.semaphore_wait(pltpu.get_barrier_semaphore(), count)


def remote(src, dst, send_sem, recv_sem, to):
    return pltpu.make_async_remote_copy(
        src_ref=src,
        dst_ref=dst,
        send_sem=send_sem,
        recv_sem=recv_sem,
        device_id=peer(to),
        device_id_type=MESH,
    )


def all_others(me):
    return [lax.rem(me + d, N_T) for d in range(1, N_T)]


class Gather:
    def __init__(self, own_ref, buf, run_of, send_sem, recv_sem):
        me = lax.axis_index("tensor")
        y = lax.rem(me, 4)
        base = me - y
        self.me = me
        self.own_ref, self.buf, self.run_of = own_ref, buf, run_of
        self.send_sem, self.recv_sem = send_sem, recv_sem
        self.up = base + lax.rem(y + 1, 4)
        self.down = base + lax.rem(y + 3, 4)
        far = base + lax.rem(y + 2, 4)

        def across(t):
            return lax.rem(t + 4, N_T)

        self.pair = across(me)
        self.owner = [
            self.down,
            self.up,
            self.pair,
            far,
            across(self.down),
            across(self.up),
            across(far),
        ]
        self.started = []

    def send(self, src, owner, kind, s, to):
        copy = remote(
            self.run_of(src, s),
            self.run_of(self.buf.at[owner], s),
            self.send_sem.at[len(self.started)],
            self.recv_sem.at[kind, s],
            to,
        )
        copy.start()
        self.started.append(copy)

    def forward(self, which, kind, s, to):
        self.send(self.buf.at[self.owner[which]], self.owner[which], kind, s, to)

    def wait(self, kind, s):
        place = self.run_of(self.buf.at[self.owner[kind]], s)
        remote(place, place, self.send_sem.at[0], self.recv_sem.at[kind, s], self.pair).wait_recv()

    def send_own(self, s):
        self.send(self.own_ref, self.me, 2, s, self.pair)
        self.send(self.own_ref, self.me, 0, s, self.up)
        self.send(self.own_ref, self.me, 1, s, self.down)

    def run(self, use, done, between):
        for s in range(SUBS):
            self.wait(0, s)
            if s % 2 == 0:
                self.forward(0, 3, s, self.up)
            self.wait(1, s)
            if s % 2 == 1:
                self.forward(1, 3, s, self.down)
            self.wait(2, s)
            self.forward(2, 4, s, self.up)
            self.forward(2, 5, s, self.down)
            if s + DEPTH < SUBS:
                self.send_own(s + DEPTH)
            for kind in (-1, 0, 1, 2):
                use(kind, s)
            if s > 0:
                for kind in (4, 5):
                    self.wait(kind, s - 1)
                    use(kind, s - 1)
            self.wait(3, s)
            self.forward(3, 6, s, self.pair)
            use(3, s)
            between(s)
            if s > 0:
                self.last(s - 1, use, done)
        for kind in (4, 5):
            self.wait(kind, SUBS - 1)
            use(kind, SUBS - 1)
        self.last(SUBS - 1, use, done)

    def last(self, s, use, done):
        self.wait(6, s)
        use(6, s)
        done(s)

    def end(self):
        for copy in self.started:
            copy.wait_send()


GATHER_SEMS = [DMA((7 * SUBS,)), DMA((7, SUBS))]
SEEN_CHIPS = 4


def put(src, dst, send_sem, recv_sem, to):
    return pltpu.make_async_remote_copy(
        src_ref=src,
        dst_ref=dst,
        send_sem=send_sem,
        recv_sem=recv_sem,
        device_id=to,
        device_id_type=MESH,
    )


def ring_of(replica):
    per = lax.axis_size("ctx")
    return {"dp": lax.div(replica, per), "ctx": lax.rem(replica, per)}


class Columns:
    def __init__(self, w_ref, all_ref, a2a_send, a2a_recv, send_sem, recv_sem, own_sem):
        self.all_ref = all_ref
        self.a2a_send, self.a2a_recv = a2a_send, a2a_recv
        self.send_sem, self.recv_sem = send_sem, recv_sem
        self.own_sem = own_sem
        self.w_ref = w_ref
        self.me = lax.axis_index("tensor")
        per = lax.axis_size("ctx")
        dp, ctx = lax.axis_index("dp"), lax.axis_index("ctx")
        core = lax.rem(ctx, 2)
        self.replica = dp * per + ctx
        sibling = ctx + 1 - 2 * core
        up, down, far = lax.rem(ctx + 2, per), lax.rem(ctx + per - 2, per), lax.rem(ctx + 4, per)
        here, there = dp * per, (1 - dp) * per
        self.to = {
            "z": {"dp": 1 - dp},
            "up": {"ctx": up},
            "down": {"ctx": down},
            "near": {"ctx": sibling},
        }
        self.piece = {
            "own": here + ctx,
            "z": there + ctx,
            "down": here + down,
            "up": here + up,
            "z down": there + down,
            "z up": there + up,
            "far": here + far,
            "z far": there + far,
        }
        self.near_piece = {}
        for name, index in self.piece.items():
            self.near_piece[name] = index + 1 - 2 * core
        self.started = []

    def block(self, t):
        piece, columns = self.all_ref.shape[2:]
        rows = pl.ds(pl.multiple_of(self.replica * piece, piece), piece)
        return self.w_ref.at[rows, pl.ds(pl.multiple_of(t * columns, columns), columns)]

    def fetch(self):
        place = self.all_ref.at[self.replica, self.me]
        self.own = pltpu.make_async_copy(self.block(self.me), place, self.own_sem)
        self.own.start()
        self.fetches = []
        for d, other in enumerate(all_others(self.me)):
            copy = remote(self.block(other), place, self.a2a_send.at[d], self.a2a_recv.at[d], other)
            copy.start()
            self.fetches.append(copy)

    def send(self, name, way, arrives):
        place = self.all_ref.at[self.piece[name]]
        copy = put(
            place,
            place,
            self.send_sem.at[len(self.started)],
            self.recv_sem.at[arrives],
            self.to[way],
        )
        copy.start()
        self.started.append(copy)

    def wait(self, index, arrives):
        place = self.all_ref.at[index]
        put(
            place, place, self.send_sem.at[0], self.recv_sem.at[arrives], self.to["near"]
        ).wait_recv()

    ARRIVES = ("z", "down", "up", "z down", "z up", "far", "z far")

    def arrived(self, name):
        self.wait(self.piece[name], self.ARRIVES.index(name))
        self.send_near(name)

    def send_near(self, name):
        self.send(name, "near", 7 + list(self.piece).index(name))

    def step(self, s):
        if s == 0:
            self.own.wait()
            for copy in self.fetches:
                copy.wait()
            self.send("own", "z", 0)
            self.send("own", "up", 1)
            self.send("own", "down", 2)
            self.send_near("own")
        if s == 1:
            self.arrived("z")
            self.send("z", "up", 3)
            self.send("z", "down", 4)
        if s == 2:
            self.arrived("down")
            self.send("down", "up", 5)
            self.arrived("up")
        if s == 3:
            self.arrived("z up")
            self.send("z up", "down", 6)
            self.arrived("z down")
            self.arrived("far")

    def end(self):
        self.arrived("z far")
        for i, name in enumerate(self.piece):
            self.wait(self.near_piece[name], 7 + i)
        for copy in self.started:
            copy.wait_send()


class Shared:
    def __init__(self, own, kv_ref, own_sem, send_sem, recv_sem, near_send, near_recv):
        per = lax.axis_size("ctx") // 2
        ctx = lax.axis_index("ctx")
        self.per = per
        self.core = lax.rem(ctx, 2)
        self.chip = lax.axis_index("dp") * per + lax.div(ctx, 2)
        self.chips = lax.axis_size("dp") * per
        self.block = self.chip * 2 + self.core
        self.sibling = {"ctx": ctx + 1 - 2 * self.core}
        self.sibling_block = self.block + 1 - 2 * self.core
        self.own, self.kv_ref, self.own_sem = own, kv_ref, own_sem
        self.send_sem, self.recv_sem = send_sem, recv_sem
        self.near_send, self.near_recv = near_send, near_recv
        step = own.shape[0] // SUBS
        self.first = [0, (SUBS - 1) * step]
        self.rows = [(SUBS - 1) * step, step]

    def run(self, ref, s):
        return ref.at[pl.ds(self.first[s], self.rows[s])]

    def to_chip(self, k, s):
        other = self.chip + k
        return put(
            self.run(self.own, s),
            self.run(self.kv_ref.at[self.block], s),
            self.send_sem.at[k - 1, s],
            self.recv_sem.at[k - 1, s],
            {"dp": lax.div(other, self.per), "ctx": lax.rem(other, self.per) * 2 + self.core},
        )

    def to_sibling(self, k, s):
        place = self.run(self.kv_ref.at[self.block - 2 * k], s)
        return put(
            self.run(self.own, s) if k == 0 else place,
            place,
            self.near_send.at[k, s],
            self.near_recv.at[k, s],
            self.sibling,
        )

    def keep(self, s):
        return pltpu.make_async_copy(
            self.run(self.own, s), self.run(self.kv_ref.at[self.block], s), self.own_sem.at[s]
        )

    def send(self, s):
        for k in (2, 1, 3, 4):

            @pl.when(self.chip + k < self.chips)
            def _(k=k):
                self.to_chip(k, s).start()

        self.to_sibling(0, s).start()
        self.keep(s).start()

    def pass_on(self, s):
        for k in (1, 3, 4, 2):

            @pl.when(self.chip - k >= 0)
            def _(k=k):
                place = self.run(self.kv_ref.at[self.block - 2 * k], s)
                put(
                    place,
                    place,
                    self.send_sem.at[k - 1, s],
                    self.recv_sem.at[k - 1, s],
                    self.sibling,
                ).wait_recv()
                self.to_sibling(k, s).start()

    def from_sibling(self, k, s):
        place = self.run(self.kv_ref.at[self.sibling_block - 2 * k], s)
        put(
            place, place, self.near_send.at[k, s], self.near_recv.at[k, s], self.sibling
        ).wait_recv()

    def end(self):
        for s in range(2):
            self.keep(s).wait()
            self.to_sibling(0, s).wait_send()
            self.from_sibling(0, s)
        for k in range(1, SEEN_CHIPS + 1):

            @pl.when(self.chip - k >= 0)
            def _(k=k):
                for s in range(2):
                    self.to_sibling(k, s).wait_send()
                    self.from_sibling(k, s)

            @pl.when(self.chip + k < self.chips)
            def _(k=k):
                for s in range(2):
                    self.to_chip(k, s).wait_send()


def project_kernel(
    tok_hbm,
    gain_hbm,
    source_hbm,
    segment_hbm,
    w_ref,
    bias_hbm,
    freq_hbm,
    wo_ref,
    q_ref,
    spots_ref,
    kv_ref,
    columns_ref,
    tok,
    gain_row,
    sources_row,
    segments_row,
    bias_row,
    freq_row,
    stats,
    docs,
    normed,
    buf,
    w_buf,
    total,
    own,
    load_sem,
    w_sem,
    stat_send,
    stat_recv,
    doc_send,
    doc_recv,
    gather_send,
    gather_recv,
    a2a_send,
    a2a_recv,
    col_send,
    col_recv,
    col_own,
    kv_own,
    kv_send,
    kv_recv,
    near_send,
    near_recv,
):
    me = lax.axis_index("tensor")
    replica = lax.axis_index("dp") * lax.axis_size("ctx") + lax.axis_index("ctx")
    replicas = docs.shape[0]
    rows, width = tok.shape
    features = width * N_T
    step = rows // SUBS
    others = all_others(me)
    alike = [ring_of(lax.rem(replica + d, replicas)) for d in range(1, replicas)]
    greet(others)
    for other in alike:
        pl.semaphore_signal(
            pltpu.get_barrier_semaphore(), inc=1, device_id=other, device_id_type=MESH
        )
    small = []
    for i, (src, dst) in enumerate(
        (
            (source_hbm, sources_row),
            (segment_hbm, segments_row),
            (gain_hbm.at[me], gain_row),
            (bias_hbm, bias_row),
            (freq_hbm, freq_row),
        )
    ):
        small.append(pltpu.make_async_copy(src, dst, load_sem.at[SUBS + i]))
        small[-1].start()
    token_loads = []
    for i in range(SUBS):
        cut = pl.ds(i * step, step)
        token_loads.append(pltpu.make_async_copy(tok_hbm.at[cut], tok.at[cut], load_sem.at[i]))
        token_loads[-1].start()
    gather = Gather(
        normed, buf, lambda ref, s: ref.at[pl.ds(s * step, step)], gather_send, gather_recv
    )
    w_loads = []
    for i, t in enumerate([me] + gather.owner):
        w_loads.append(
            pltpu.make_async_copy(
                w_ref.at[pl.ds(pl.multiple_of(t * width, width), width)], w_buf.at[i], w_sem.at[i]
            )
        )
        w_loads[-1].start()

    for copy in small:
        copy.wait()
    sources = sources_row[...]
    segments = segments_row[...]
    row = replica * rows + lax.broadcasted_iota(jnp.int32, (1, rows), 1)
    none = rows * replicas
    lane = lax.broadcasted_iota(jnp.int32, (8, 128), 1)
    line = lax.broadcasted_iota(jnp.int32, (8, 128), 0)
    table = jnp.full((8, 128), none, jnp.int32)
    for doc in range(DOC_IDS):
        of_doc = segments == doc
        first_source = jnp.min(jnp.where(of_doc, sources, none), axis=1, keepdims=True)
        first_packed = jnp.min(jnp.where(of_doc, row, none), axis=1, keepdims=True)
        found = jnp.where(line == 0, first_source, first_packed)
        table = jnp.where(lane == doc, found, table)
    docs[pl.ds(replica, 1)] = table[None]
    for i in range(SUBS):
        token_loads[i].wait()
        squares = jnp.zeros((step, 128), jnp.float32)
        for j in range(width // 128):
            part = tok[i * step : (i + 1) * step, j * 128 : (j + 1) * 128].astype(jnp.float32)
            squares = squares + part * part
        summed = jnp.sum(squares.T, axis=0, keepdims=True)
        stats[pl.ds(me, 1), :, i * step : (i + 1) * step] = jnp.broadcast_to(
            summed[None], (1, 8, step)
        )
    greeted(N_T - 1 + replicas - 1)

    stat_copies = []
    for d, other in enumerate(others):
        stat_copies.append(
            remote(stats.at[me], stats.at[me], stat_send.at[d], stat_recv.at[d], other)
        )
        stat_copies[-1].start()
    doc_copies = []
    for d, other in enumerate(alike):
        place = docs.at[replica]
        doc_copies.append(put(place, place, doc_send.at[d], doc_recv.at[d], other))
        doc_copies[-1].start()
    columns = Columns(wo_ref, columns_ref, a2a_send, a2a_recv, col_send, col_recv, col_own)
    columns.fetch()
    for copy in stat_copies:
        copy.wait()
    summed = stats[0]
    for t in range(1, N_T):
        summed = summed + stats[t]
    scale = lax.rsqrt(summed[0:1] * (1.0 / features) + 1e-06)
    for i in range(SUBS):
        along = jnp.broadcast_to(scale[:, i * step : (i + 1) * step], (128, step)).T
        for j in range(width // 128):
            cut = (slice(i * step, (i + 1) * step), slice(j * 128, (j + 1) * 128))
            gain = gain_row[:, j * 128 : (j + 1) * 128]
            normed[cut] = (tok[cut].astype(jnp.float32) * along * gain).astype(jnp.bfloat16)

    shared = Shared(own, kv_ref, kv_own, kv_send, kv_recv, near_send, near_recv)
    spots = {}

    def find_spots():
        for copy in doc_copies:
            copy.wait()
        table = docs[0]
        for r in range(1, replicas):
            table = jnp.minimum(table, docs[r])
        start = jnp.full((1, rows), -1, jnp.int32)
        place = row
        for doc in range(DOC_IDS):
            first_source = table[0:1, doc : doc + 1]
            first_packed = table[1:2, doc : doc + 1]
            later = (first_source <= row) & (first_source > start)
            start = jnp.where(later, first_source, start)
            place = jnp.where(later, row + (first_packed - first_source), place)
        spots_ref[...] = jnp.where(
            lax.broadcasted_iota(jnp.int32, (8, rows), 0) == 0, start, place
        )
        spots["position"] = lax.rem(place, PACK).astype(jnp.float32)

    def use(kind, s):
        i = kind + 1
        if s == 0:
            w_loads[i].wait()
        chunk = normed if kind < 0 else buf.at[gather.owner[kind]]
        here = slice(s * step, (s + 1) * step)
        term = jnp.dot(chunk[here, :], w_buf[i], preferred_element_type=jnp.float32)
        if kind < 0:
            total[here, :] = term
        else:
            total[here, :] += term

    def done(s):
        here = slice(s * step, (s + 1) * step)
        bias = bias_row[...].astype(jnp.float32)
        angle = (
            jnp.broadcast_to(spots["position"][:, here], (128, step)).T * freq_row[...]
        )
        cosine = jnp.cos(angle)
        sine = jnp.sin(angle)
        first = lax.broadcasted_iota(jnp.int32, (step, HD), 1) < HD // 2
        sine = jnp.where(first, -sine, sine)

        def slot(index):
            cut = slice(index * HD, (index + 1) * HD)
            return (total[here, cut] + bias[:, cut]).astype(jnp.bfloat16)

        def turned(index):
            wide = slot(index).astype(jnp.float32)
            return (wide * cosine + pltpu.roll(wide, HD // 2, 1) * sine).astype(jnp.bfloat16)

        own[here, :HD] = turned(GROUP)
        own[here, HD:] = slot(GROUP + 1)
        if s >= SUBS - 2:
            shared.send(s - SUBS + 2)
        for head in range(GROUP):
            q_ref[here, head * HD : (head + 1) * HD] = turned(head)

    for s in range(DEPTH):
        gather.send_own(s)
    find_spots()
    gather.run(use, done, columns.step)
    shared.pass_on(0)
    columns.end()
    shared.pass_on(1)
    shared.end()
    gather.end()


def project(tokens, gain, sources, segments, weight, bias, out_weight, replicas):
    rows, width = tokens.shape
    columns = weight.shape[1]
    depth, out_width = out_weight.shape
    half = HD // 2
    freqs = (1e6 ** (-(np.arange(half) * 2.0) / HD)).astype(np.float32)
    freqs = jnp.asarray(np.concatenate([freqs, freqs])[None])
    hbm = pl.BlockSpec(memory_space=pltpu.HBM)
    vmem = pl.BlockSpec(memory_space=VMEM)
    return pl.pallas_call(
        project_kernel,
        out_shape=(
            jax.ShapeDtypeStruct((rows, GROUP * HD), jnp.bfloat16),
            jax.ShapeDtypeStruct((8, rows), jnp.int32),
            jax.ShapeDtypeStruct((replicas, rows, 2 * HD), jnp.bfloat16),
            jax.ShapeDtypeStruct((replicas, N_T, depth // replicas, out_width // N_T), jnp.bfloat16),
        ),
        in_specs=[hbm] * 8,
        out_specs=(vmem, vmem, hbm, hbm),
        scratch_shapes=[
            VMEM((rows, width), jnp.bfloat16),
            VMEM((1, width), jnp.float32),
            VMEM((1, rows), jnp.int32),
            VMEM((1, rows), jnp.int32),
            VMEM((1, columns), jnp.bfloat16),
            VMEM((1, HD), jnp.float32),
            VMEM((N_T, 8, rows), jnp.float32),
            VMEM((replicas, 8, 128), jnp.int32),
            VMEM((rows, width), jnp.bfloat16),
            VMEM((N_T, rows, width), jnp.bfloat16),
            VMEM((N_T, width, columns), jnp.bfloat16),
            VMEM((rows, columns), jnp.float32),
            VMEM((rows, 2 * HD), jnp.bfloat16),
            DMA((SUBS + 5,)),
            DMA((N_T,)),
            DMA((N_T - 1,)),
            DMA((N_T - 1,)),
            DMA((replicas - 1,)),
            DMA((replicas - 1,)),
            *GATHER_SEMS,
            DMA((N_T - 1,)),
            DMA((N_T - 1,)),
            DMA((15,)),
            DMA((15,)),
            DMA,
            DMA((2,)),
            DMA((SEEN_CHIPS, 2)),
            DMA((SEEN_CHIPS, 2)),
            DMA((SEEN_CHIPS + 1, 2)),
            DMA((SEEN_CHIPS + 1, 2)),
        ],
        compiler_params=pltpu.CompilerParams(
            collective_id=1, has_side_effects=True, vmem_limit_bytes=58 * 2**20
        ),
        cost_estimate=pl.CostEstimate(
            flops=2 * rows * width * N_T * columns, bytes_accessed=10**8, transcendentals=10**5
        ),
    )(
        tokens,
        gain.reshape(N_T, 1, width),
        sources.reshape(1, rows),
        segments.reshape(1, rows),
        weight,
        bias,
        freqs,
        out_weight,
    )


def output_kernel(
    own_ref,
    w_ref,
    out_ref,
    buf,
    w_buf,
    total,
    ready,
    gather_send,
    gather_recv,
    w_sem,
    out_send,
    out_recv,
    own_sem,
):
    me = lax.axis_index("tensor")
    part = own_ref.shape[1] // SUBS
    others = all_others(me)
    greet(others)

    def run_of(ref, s):
        return ref.at[:, pl.ds(s * part, part)]

    gather = Gather(own_ref, buf, run_of, gather_send, gather_recv)
    loads = []
    for i, t in enumerate([me] + gather.owner):
        loads.append(pltpu.make_async_copy(w_ref.at[:, t], w_buf.at[i], w_sem.at[i]))
        loads[-1].start()
    greeted(N_T - 1)
    depth = own_ref.shape[2]
    columns = total.shape[1]
    place = pl.ds(pl.multiple_of(me * columns, columns), columns)
    copies = []

    def use(kind, s):
        i = kind + 1
        if s == 0:
            loads[i].wait()
        chunk = own_ref if kind < 0 else buf.at[gather.owner[kind]]
        weight = w_buf[i].reshape(depth, columns)
        rows = chunk[:, s * part : (s + 1) * part, :].reshape(N_T * part, depth)
        term = jnp.dot(rows, weight, preferred_element_type=jnp.float32)
        term = term.astype(jnp.bfloat16).astype(jnp.float32)
        here = slice(s * N_T * part, (s + 1) * N_T * part)
        if kind < 0:
            total[here, :] = term
        else:
            total[here, :] += term

    def done(s):
        here = slice(s * N_T * part, (s + 1) * N_T * part)
        ready[s] = total[here, :].astype(jnp.bfloat16).reshape(N_T, part, columns)
        target = out_ref.at[pl.ds(s * part, part), place]
        for d, other in enumerate(others):
            copies.append(
                remote(ready.at[s, other], target, out_send.at[d, s], out_recv.at[d, s], other)
            )
            copies[-1].start()
        copies.append(pltpu.make_async_copy(ready.at[s, me], target, own_sem.at[s]))
        copies[-1].start()

    for s in range(DEPTH):
        gather.send_own(s)
    gather.run(use, done, lambda s: None)
    for copy in copies:
        copy.wait()
    gather.end()


def project_out(attended, weight):
    rows, depth = attended.shape
    columns = weight.shape[3]
    each = rows // N_T
    return pl.pallas_call(
        output_kernel,
        out_shape=jax.ShapeDtypeStruct((each, columns * N_T), jnp.bfloat16),
        in_specs=[pl.BlockSpec(memory_space=VMEM), pl.BlockSpec(memory_space=pltpu.HBM)],
        out_specs=pl.BlockSpec(memory_space=pltpu.HBM),
        scratch_shapes=[
            VMEM((N_T, N_T, each, depth), jnp.bfloat16),
            VMEM((N_T, weight.shape[0], weight.shape[2], columns), jnp.bfloat16),
            VMEM((rows, columns), jnp.float32),
            VMEM((SUBS, N_T, each // SUBS, columns), jnp.bfloat16),
            *GATHER_SEMS,
            DMA((N_T,)),
            DMA((N_T - 1, SUBS)),
            DMA((N_T - 1, SUBS)),
            DMA((SUBS,)),
        ],
        compiler_params=pltpu.CompilerParams(
            collective_id=3, has_side_effects=True, vmem_limit_bytes=48 * 2**20
        ),
        cost_estimate=pl.CostEstimate(
            flops=2 * rows * depth * N_T * columns, bytes_accessed=10**8, transcendentals=0
        ),
    )(attended.reshape(N_T, each, depth), weight)


TILE_Q = 256
SEEN_BLOCKS = 2 * SEEN_CHIPS
TILE_K = 256
LOW = -1e30


def attend_kernel(
    spots_hbm, q_hbm, kv_hbm, out_ref, starts, spots_ref, q_ref, kv_ref, load_sem, kv_sem
):
    rows = q_ref.shape[0]
    block = lax.axis_index("dp") * lax.axis_size("ctx") + lax.axis_index("ctx")
    first_row = block * rows
    loads = [
        pltpu.make_async_copy(spots_hbm, starts, load_sem.at[0]),
        pltpu.make_async_copy(spots_hbm, spots_ref, load_sem.at[1]),
        pltpu.make_async_copy(q_hbm, q_ref, load_sem.at[2]),
    ]
    for load in loads:
        load.start()

    def kv_load(back):
        return pltpu.make_async_copy(
            kv_hbm.at[block - back],
            kv_ref.at[pl.ds(pl.multiple_of((block - back) * rows, rows), rows)],
            kv_sem.at[back],
        )

    for back in range(SEEN_BLOCKS + 1):

        @pl.when(block - back >= 0)
        def _(back=back):
            kv_load(back).start()

    for load in loads:
        load.wait()
    for back in range(SEEN_BLOCKS + 1):

        @pl.when(block - back >= 0)
        def _(back=back):
            kv_load(back).wait()

    heads = q_ref.shape[1] // HD
    factor = HD**-0.5 * 1.4426950408889634
    for a in range(rows // TILE_Q):
        base = first_row + a * TILE_Q
        start = spots_ref[0:1, a * TILE_Q : (a + 1) * TILE_Q]
        query_row = base + lax.broadcasted_iota(jnp.int32, (1, TILE_Q), 1)
        low_tile = lax.div(starts[0, a * TILE_Q], TILE_K)
        high_tile = lax.div(base + TILE_Q, TILE_K)

        def one(i, carry, a=a, start=start, query_row=query_row, high_tile=high_tile):
            tile = high_tile - 1 - i
            cut = pl.ds(pl.multiple_of(tile * TILE_K, TILE_K), TILE_K)
            keys = kv_ref[cut, :HD]
            values = kv_ref[cut, HD:].T
            key_row = tile * TILE_K + lax.broadcasted_iota(jnp.int32, (TILE_K, TILE_Q), 0)
            allowed = (key_row >= start) & (key_row <= query_row)
            after = []
            for h in range(heads):
                top, denominator, weighted = carry[h]
                query = q_ref[a * TILE_Q : (a + 1) * TILE_Q, h * HD : (h + 1) * HD]
                scores = lax.dot_general(
                    keys, query, (((1,), (1,)), ((), ())), preferred_element_type=jnp.float32
                )
                scores = jnp.where(allowed, scores * factor, 2 * LOW)
                new_top = jnp.maximum(top, jnp.max(scores, axis=0, keepdims=True))
                weights = jnp.exp2(scores - new_top)
                shrink = jnp.exp2(top - new_top)
                denominator = denominator * shrink + jnp.sum(weights, axis=0, keepdims=True)
                coarse = weights.astype(jnp.bfloat16)
                fine = (weights - coarse.astype(jnp.float32)).astype(jnp.bfloat16)
                weighted = weighted * shrink
                weighted += jnp.dot(values, coarse, preferred_element_type=jnp.float32)
                weighted += jnp.dot(values, fine, preferred_element_type=jnp.float32)
                after.append((new_top, denominator, weighted))
            return tuple(after)

        begin = (
            jnp.full((1, TILE_Q), LOW, jnp.float32),
            jnp.zeros((1, TILE_Q), jnp.float32),
            jnp.zeros((HD, TILE_Q), jnp.float32),
        )
        ended = lax.fori_loop(0, high_tile - low_tile, one, (begin,) * heads)
        for h in range(heads):
            _, denominator, weighted = ended[h]
            out_ref[a * TILE_Q : (a + 1) * TILE_Q, h * HD : (h + 1) * HD] = (
                (weighted / denominator).T.astype(jnp.bfloat16)
            )


def attend(spots, queries, both):
    blocks, rows, width = both.shape
    hbm = pl.BlockSpec(memory_space=pltpu.HBM)
    return pl.pallas_call(
        attend_kernel,
        out_shape=jax.ShapeDtypeStruct(queries.shape, jnp.bfloat16),
        in_specs=[hbm, hbm, hbm],
        out_specs=pl.BlockSpec(memory_space=VMEM),
        scratch_shapes=[
            pltpu.SMEM(spots.shape, jnp.int32),
            VMEM(spots.shape, jnp.int32),
            VMEM(queries.shape, jnp.bfloat16),
            VMEM((blocks * rows, width), jnp.bfloat16),
            DMA((3,)),
            DMA((SEEN_BLOCKS + 1,)),
        ],
        compiler_params=pltpu.CompilerParams(vmem_limit_bytes=58 * 2**20),
        cost_estimate=pl.CostEstimate(flops=10**9, bytes_accessed=10**7, transcendentals=10**7),
    )(spots, queries, both)


def per_device(
    tokens, norm_gain, project_weight, project_bias, output_weight, source_row, segment_id
):
    replicas = lax.axis_size("dp") * lax.axis_size("ctx")
    flat_weight = project_weight.reshape(project_weight.shape[0], -1)
    queries, spots, both, out_columns = project(
        tokens, norm_gain, source_row, segment_id, flat_weight, project_bias, output_weight, replicas
    )
    attended = attend(spots, queries, both)
    return project_out(attended, out_columns)


def solution(mesh):
    placed = (
        P(("dp", "ctx"), "tensor"),
        P(),
        P(None, "tensor", None),
        P("tensor", None),
        P("tensor", None),
        P(("dp", "ctx")),
        P(("dp", "ctx")),
    )
    return jax.shard_map(
        per_device,
        mesh=mesh,
        in_specs=placed,
        out_specs=P(("dp", "ctx", "tensor"), None),
        check_vma=False,
    )
```

time: 561 us -> 176 us (0.31)
  the two profiles are of different devices: /device:TPU:32 before, /device:TPU:5 now
where the time goes in v3:
time: 176 us
  Pallas kernels  174 us (99%)
  local copies, waits for them, and re-layouts  2.01 us (1%)
    pallas_call x1, Pallas kernels, project(): pl.pallas_call(project_kernel, out_shape=(jax.ShapeDtypeStruct((rows, GRO...  91.4 us
    pallas_call x1, Pallas kernels, project_out(): pl.pallas_call(output_kernel, out_shape=jax.ShapeDtypeStruct((each, colum...  62.8 us
    pallas_call x1, Pallas kernels, attend(): pl.pallas_call(attend_kernel, out_shape=jax.ShapeDtypeStruct(queries.shap...  20 us

profile of v3, /device:TPU:5, one launch (start us, length us, event | category | flops | bytes accessed | tf_op | source)
XLA Modules:
  0.0 176.2 jit_solution(5317169616352035120)
XLA Ops:
  0.0 91.4 %shard_map.82 = (bf16[512,512]{1,0:T(8,128)(2,1)}, s32[8,512]{1,0:T(8,128)}, bf16[16,512,256]{2,1,0:T(8,128)(2,1)}, bf16[16,8,32,1024]{3,2,1,0:T(8,128)(2,1)}) custom-call(bf16[512,1024]{1,0:T(8,128)(2,1)} %tok_hbm.1, f32[8,1,1024]{2,1,0:T(1,128)} %bitcast.7, s32[1,512]{1,0:T(1,128)} %bitcast.8, s32[1,512]{1,0:T(1,128)} %bitcast.9, ...), custom_call_target="tpu_custom_call" | custom-call | flops 6442450944 | bytes 100000000 | tf_op jit(solution)/shard_map/pallas_call | solution.py:586
  91.4 20.0 %shard_map.83 = bf16[512,512]{1,0:T(8,128)(2,1)} custom-call(s32[8,512]{1,0:T(8,128)} %get-tuple-element.9.spots_hbm, bf16[512,512]{1,0:T(8,128)(2,1)} %get-tuple-element.10.q_hbm, bf16[16,512,256]{2,1,0:T(8,128)(2,1)} %get-tuple-element.11.kv_hbm), custom_call_target="tpu_custom_call" | custom-call | flops 1000000000 | bytes 10000000 | tf_op jit(solution)/shard_map/pallas_call | solution.py:837
  111.3 0.0 copy-start
  111.4 1.0 copy-done
  112.4 62.8 %shard_map.84 = bf16[64,8192]{1,0:T(8,128)(2,1)S(1)} custom-call(bf16[8,64,512]{2,1,0:T(8,128)(2,1)S(1)} %bitcast.5, bf16[16,8,32,1024]{3,2,1,0:T(8,128)(2,1)} %get-tuple-element.12.w_ref), custom_call_target="tpu_custom_call" | custom-call | flops 4294967296 | bytes 100000000 | tf_op jit(solution)/shard_map/pallas_call | solution.py:719
  175.2 1.0 copy.10
Async XLA Ops:
  111.3 1.0 copy-start

commit v4 on v3

--- a/solution.py
+++ b/solution.py
@@ -13,6 +13,10 @@
 N_T = 8
 SUBS = 4
 DEPTH = 2
+CUTS = (0, 128, 256, 384, 512)
+OVER_Z = ((), ())
+OUT_OVER_Z = ((1,), (2,))
+BATCHES = ((0, 2), (2, 3), (3, 4))
 MESH = pl.DeviceIdType.MESH
 VMEM = pltpu.VMEM
 DMA = pltpu.SemaphoreType.DMA
@@ -48,7 +52,8 @@
 
 
 class Gather:
-    def __init__(self, own_ref, buf, run_of, send_sem, recv_sem):
+    def __init__(self, own_ref, buf, run_of, send_sem, recv_sem, over_z=((), ())):
+        self.over_z = over_z
         me = lax.axis_index("tensor")
         y = lax.rem(me, 4)
         base = me - y
@@ -102,30 +107,38 @@
             self.wait(0, s)
             if s % 2 == 0:
                 self.forward(0, 3, s, self.up)
+            if s in self.over_z[0]:
+                self.forward(0, 4, s, self.pair)
             self.wait(1, s)
             if s % 2 == 1:
                 self.forward(1, 3, s, self.down)
+            if s in self.over_z[1]:
+                self.forward(1, 5, s, self.pair)
             self.wait(2, s)
-            self.forward(2, 4, s, self.up)
-            self.forward(2, 5, s, self.down)
+            if s not in self.over_z[0]:
+                self.forward(2, 4, s, self.up)
+            if s not in self.over_z[1]:
+                self.forward(2, 5, s, self.down)
             if s + DEPTH < SUBS:
                 self.send_own(s + DEPTH)
             for kind in (-1, 0, 1, 2):
                 use(kind, s)
             if s > 0:
-                for kind in (4, 5):
-                    self.wait(kind, s - 1)
-                    use(kind, s - 1)
+                self.across_sides(s - 1, use)
             self.wait(3, s)
             self.forward(3, 6, s, self.pair)
             use(3, s)
             between(s)
             if s > 0:
                 self.last(s - 1, use, done)
-        for kind in (4, 5):
-            self.wait(kind, SUBS - 1)
-            use(kind, SUBS - 1)
+        self.across_sides(SUBS - 1, use)
         self.last(SUBS - 1, use, done)
+
+    def across_sides(self, s, use):
+        self.wait(4, s)
+        use(4, s)
+        self.wait(5, s)
+        use(5, s)
 
     def last(self, s, use, done):
         self.wait(6, s)
@@ -267,7 +280,7 @@
 
 
 class Shared:
-    def __init__(self, own, kv_ref, own_sem, send_sem, recv_sem, near_send, near_recv):
+    def __init__(self, own, kv_ref, own_sem, send_sem, recv_sem, near_send, near_recv, along_send):
         per = lax.axis_size("ctx") // 2
         ctx = lax.axis_index("ctx")
         self.per = per
@@ -280,12 +293,12 @@
         self.own, self.kv_ref, self.own_sem = own, kv_ref, own_sem
         self.send_sem, self.recv_sem = send_sem, recv_sem
         self.near_send, self.near_recv = near_send, near_recv
-        step = own.shape[0] // SUBS
-        self.first = [0, (SUBS - 1) * step]
-        self.rows = [(SUBS - 1) * step, step]
+        self.along_send = along_send
+        self.x = lax.rem(self.chip, per)
 
     def run(self, ref, s):
-        return ref.at[pl.ds(self.first[s], self.rows[s])]
+        first, last = (CUTS[cut] for cut in BATCHES[s])
+        return ref.at[pl.ds(first, last - first)]
 
     def to_chip(self, k, s):
         other = self.chip + k
@@ -312,18 +325,41 @@
             self.run(self.own, s), self.run(self.kv_ref.at[self.block], s), self.own_sem.at[s]
         )
 
+    def sends(self, act):
+        for k in (2, 1, 3):
+
+            @pl.when(self.x + k < self.per)
+            def _(k=k):
+                act(k)
+
+        @pl.when(self.chip + self.per < self.chips)
+        def _():
+            act(self.per)
+
     def send(self, s):
-        for k in (2, 1, 3, 4):
-
-            @pl.when(self.chip + k < self.chips)
-            def _(k=k):
-                self.to_chip(k, s).start()
-
+        self.sends(lambda k: self.to_chip(k, s).start())
         self.to_sibling(0, s).start()
         self.keep(s).start()
 
+    def along(self, m, s):
+        place = self.run(self.kv_ref.at[self.block - 2 * self.per], s)
+        return put(
+            place,
+            place,
+            self.along_send.at[m - 1, s],
+            self.recv_sem.at[self.per - m - 1, s],
+            {"ctx": (self.x - m) * 2 + self.core},
+        )
+
+    def relays(self, act):
+        for m in (2, 1, 3):
+
+            @pl.when((self.chip >= self.per) & (self.x >= m))
+            def _(m=m):
+                act(m)
+
     def pass_on(self, s):
-        for k in (1, 3, 4, 2):
+        for k in (4, 1, 3, 2):
 
             @pl.when(self.chip - k >= 0)
             def _(k=k):
@@ -335,6 +371,12 @@
                     self.recv_sem.at[k - 1, s],
                     self.sibling,
                 ).wait_recv()
+
+            if k == self.per:
+                self.relays(lambda m: self.along(m, s).start())
+
+            @pl.when(self.chip - k >= 0)
+            def _(k=k):
                 self.to_sibling(k, s).start()
 
     def from_sibling(self, k, s):
@@ -344,7 +386,7 @@
         ).wait_recv()
 
     def end(self):
-        for s in range(2):
+        for s in range(len(BATCHES)):
             self.keep(s).wait()
             self.to_sibling(0, s).wait_send()
             self.from_sibling(0, s)
@@ -352,14 +394,13 @@
 
             @pl.when(self.chip - k >= 0)
             def _(k=k):
-                for s in range(2):
+                for s in range(len(BATCHES)):
                     self.to_sibling(k, s).wait_send()
                     self.from_sibling(k, s)
 
-            @pl.when(self.chip + k < self.chips)
-            def _(k=k):
-                for s in range(2):
-                    self.to_chip(k, s).wait_send()
+        for s in range(len(BATCHES)):
+            self.sends(lambda k, s=s: self.to_chip(k, s).wait_send())
+            self.relays(lambda m, s=s: self.along(m, s).wait_send())
 
 
 def project_kernel(
@@ -376,13 +417,16 @@
     kv_ref,
     columns_ref,
     tok,
-    gain_row,
+    gain_rows,
     sources_row,
     segments_row,
     bias_row,
     freq_row,
     stats,
     docs,
+    scales,
+    cosines,
+    sines,
     normed,
     buf,
     w_buf,
@@ -406,6 +450,7 @@
     kv_recv,
     near_send,
     near_recv,
+    along_send,
 ):
     me = lax.axis_index("tensor")
     replica = lax.axis_index("dp") * lax.axis_size("ctx") + lax.axis_index("ctx")
@@ -425,7 +470,7 @@
         (
             (source_hbm, sources_row),
             (segment_hbm, segments_row),
-            (gain_hbm.at[me], gain_row),
+            (gain_hbm, gain_rows),
             (bias_hbm, bias_row),
             (freq_hbm, freq_row),
         )
@@ -437,9 +482,11 @@
         cut = pl.ds(i * step, step)
         token_loads.append(pltpu.make_async_copy(tok_hbm.at[cut], tok.at[cut], load_sem.at[i]))
         token_loads[-1].start()
-    gather = Gather(
-        normed, buf, lambda ref, s: ref.at[pl.ds(s * step, step)], gather_send, gather_recv
-    )
+
+    def run_of(ref, s):
+        return ref.at[pl.ds(CUTS[s], CUTS[s + 1] - CUTS[s])]
+
+    gather = Gather(tok, buf, run_of, gather_send, gather_recv, OVER_Z)
     w_loads = []
     for i, t in enumerate([me] + gather.owner):
         w_loads.append(
@@ -488,6 +535,8 @@
         place = docs.at[replica]
         doc_copies.append(put(place, place, doc_send.at[d], doc_recv.at[d], other))
         doc_copies[-1].start()
+    for s in range(DEPTH):
+        gather.send_own(s)
     columns = Columns(wo_ref, columns_ref, a2a_send, a2a_recv, col_send, col_recv, col_own)
     columns.fetch()
     for copy in stat_copies:
@@ -497,15 +546,10 @@
         summed = summed + stats[t]
     scale = lax.rsqrt(summed[0:1] * (1.0 / features) + 1e-06)
     for i in range(SUBS):
-        along = jnp.broadcast_to(scale[:, i * step : (i + 1) * step], (128, step)).T
-        for j in range(width // 128):
-            cut = (slice(i * step, (i + 1) * step), slice(j * 128, (j + 1) * 128))
-            gain = gain_row[:, j * 128 : (j + 1) * 128]
-            normed[cut] = (tok[cut].astype(jnp.float32) * along * gain).astype(jnp.bfloat16)
-
-    shared = Shared(own, kv_ref, kv_own, kv_send, kv_recv, near_send, near_recv)
-    spots = {}
-
+        here = slice(i * step, (i + 1) * step)
+        scales[here, :] = jnp.broadcast_to(scale[:, here], (128, step)).T
+
+    shared = Shared(own, kv_ref, kv_own, kv_send, kv_recv, near_send, near_recv, along_send)
     def find_spots():
         for copy in doc_copies:
             copy.wait()
@@ -523,30 +567,38 @@
         spots_ref[...] = jnp.where(
             lax.broadcasted_iota(jnp.int32, (8, rows), 0) == 0, start, place
         )
-        spots["position"] = lax.rem(place, PACK).astype(jnp.float32)
+        position = lax.rem(place, PACK).astype(jnp.float32)
+        first = lax.broadcasted_iota(jnp.int32, (step, HD), 1) < HD // 2
+        for i in range(SUBS):
+            here = slice(i * step, (i + 1) * step)
+            angle = jnp.broadcast_to(position[:, here], (128, step)).T * freq_row[...]
+            cosines[here, :] = jnp.cos(angle)
+            sine = jnp.sin(angle)
+            sines[here, :] = jnp.where(first, -sine, sine)
 
     def use(kind, s):
         i = kind + 1
         if s == 0:
             w_loads[i].wait()
-        chunk = normed if kind < 0 else buf.at[gather.owner[kind]]
-        here = slice(s * step, (s + 1) * step)
-        term = jnp.dot(chunk[here, :], w_buf[i], preferred_element_type=jnp.float32)
+        owner = me if kind < 0 else gather.owner[kind]
+        chunk = tok if kind < 0 else buf.at[owner]
+        here = slice(CUTS[s], CUTS[s + 1])
+        along = scales[here, :]
+        for j in range(width // 128):
+            cut = slice(j * 128, (j + 1) * 128)
+            wide = chunk[here, cut].astype(jnp.float32)
+            normed[here, cut] = (wide * along * gain_rows[owner, :, cut]).astype(jnp.bfloat16)
+        term = jnp.dot(normed[here, :], w_buf[i], preferred_element_type=jnp.float32)
         if kind < 0:
             total[here, :] = term
         else:
             total[here, :] += term
 
     def done(s):
-        here = slice(s * step, (s + 1) * step)
+        here = slice(CUTS[s], CUTS[s + 1])
         bias = bias_row[...].astype(jnp.float32)
-        angle = (
-            jnp.broadcast_to(spots["position"][:, here], (128, step)).T * freq_row[...]
-        )
-        cosine = jnp.cos(angle)
-        sine = jnp.sin(angle)
-        first = lax.broadcasted_iota(jnp.int32, (step, HD), 1) < HD // 2
-        sine = jnp.where(first, -sine, sine)
+        cosine = cosines[here, :]
+        sine = sines[here, :]
 
         def slot(index):
             cut = slice(index * HD, (index + 1) * HD)
@@ -558,18 +610,18 @@
 
         own[here, :HD] = turned(GROUP)
         own[here, HD:] = slot(GROUP + 1)
-        if s >= SUBS - 2:
-            shared.send(s - SUBS + 2)
+        for batch, (_, end) in enumerate(BATCHES):
+            if end == s + 1:
+                shared.send(batch)
         for head in range(GROUP):
             q_ref[here, head * HD : (head + 1) * HD] = turned(head)
 
-    for s in range(DEPTH):
-        gather.send_own(s)
     find_spots()
     gather.run(use, done, columns.step)
     shared.pass_on(0)
+    shared.pass_on(1)
     columns.end()
-    shared.pass_on(1)
+    shared.pass_on(2)
     shared.end()
     gather.end()
 
@@ -595,13 +647,16 @@
         out_specs=(vmem, vmem, hbm, hbm),
         scratch_shapes=[
             VMEM((rows, width), jnp.bfloat16),
-            VMEM((1, width), jnp.float32),
+            VMEM((N_T, 1, width), jnp.float32),
             VMEM((1, rows), jnp.int32),
             VMEM((1, rows), jnp.int32),
             VMEM((1, columns), jnp.bfloat16),
             VMEM((1, HD), jnp.float32),
             VMEM((N_T, 8, rows), jnp.float32),
             VMEM((replicas, 8, 128), jnp.int32),
+            VMEM((rows, HD), jnp.float32),
+            VMEM((rows, HD), jnp.float32),
+            VMEM((rows, HD), jnp.float32),
             VMEM((rows, width), jnp.bfloat16),
             VMEM((N_T, rows, width), jnp.bfloat16),
             VMEM((N_T, width, columns), jnp.bfloat16),
@@ -619,11 +674,12 @@
             DMA((15,)),
             DMA((15,)),
             DMA,
-            DMA((2,)),
-            DMA((SEEN_CHIPS, 2)),
-            DMA((SEEN_CHIPS, 2)),
-            DMA((SEEN_CHIPS + 1, 2)),
-            DMA((SEEN_CHIPS + 1, 2)),
+            DMA((len(BATCHES),)),
+            DMA((SEEN_CHIPS, len(BATCHES))),
+            DMA((SEEN_CHIPS, len(BATCHES))),
+            DMA((SEEN_CHIPS + 1, len(BATCHES))),
+            DMA((SEEN_CHIPS + 1, len(BATCHES))),
+            DMA((SEEN_CHIPS - 1, len(BATCHES))),
         ],
         compiler_params=pltpu.CompilerParams(
             collective_id=1, has_side_effects=True, vmem_limit_bytes=58 * 2**20
@@ -666,7 +722,7 @@
     def run_of(ref, s):
         return ref.at[:, pl.ds(s * part, part)]
 
-    gather = Gather(own_ref, buf, run_of, gather_send, gather_recv)
+    gather = Gather(own_ref, buf, run_of, gather_send, gather_recv, OUT_OVER_Z)
     loads = []
     for i, t in enumerate([me] + gather.owner):
         loads.append(pltpu.make_async_copy(w_ref.at[:, t], w_buf.at[i], w_sem.at[i]))

time: 176 us -> 166 us (0.943)
  the two profiles are of different devices: /device:TPU:5 before, /device:TPU:32 now
where the time goes in v4:
time: 166 us
  Pallas kernels  164 us (99%)
  local copies, waits for them, and re-layouts  2.01 us (1%)
    pallas_call x1, Pallas kernels, project(): pl.pallas_call(project_kernel, out_shape=(jax.ShapeDtypeStruct((rows, GRO...  102 us
    pallas_call x1, Pallas kernels, project_out(): pl.pallas_call(output_kernel, out_shape=jax.ShapeDtypeStruct((each, colum...  55.8 us
    pallas_call x1, Pallas kernels, attend(): pl.pallas_call(attend_kernel, out_shape=jax.ShapeDtypeStruct(queries.shap...  6.38 us

profile of v4, /device:TPU:32, one launch (start us, length us, event | category | flops | bytes accessed | tf_op | source)
XLA Modules:
  0.0 166.1 jit_solution(9506573190532413636)
XLA Ops:
  0.0 101.9 %shard_map.82 = (bf16[512,512]{1,0:T(8,128)(2,1)}, s32[8,512]{1,0:T(8,128)}, bf16[16,512,256]{2,1,0:T(8,128)(2,1)}, bf16[16,8,32,1024]{3,2,1,0:T(8,128)(2,1)}) custom-call(bf16[512,1024]{1,0:T(8,128)(2,1)} %tok_hbm.1, f32[8,1,1024]{2,1,0:T(1,128)} %bitcast.7, s32[1,512]{1,0:T(1,128)} %bitcast.8, s32[1,512]{1,0:T(1,128)} %bitcast.9, ...), custom_call_target="tpu_custom_call" | custom-call | flops 6442450944 | bytes 100000000 | tf_op jit(solution)/shard_map/pallas_call | solution.py:638
  101.9 6.4 %shard_map.83 = bf16[512,512]{1,0:T(8,128)(2,1)} custom-call(s32[8,512]{1,0:T(8,128)} %get-tuple-element.9.spots_hbm, bf16[512,512]{1,0:T(8,128)(2,1)} %get-tuple-element.10.q_hbm, bf16[16,512,256]{2,1,0:T(8,128)(2,1)} %get-tuple-element.11.kv_hbm), custom_call_target="tpu_custom_call" | custom-call | flops 1000000000 | bytes 10000000 | tf_op jit(solution)/shard_map/pallas_call | solution.py:893
  108.3 0.0 copy-start
  108.3 1.0 copy-done
  109.4 55.8 %shard_map.84 = bf16[64,8192]{1,0:T(8,128)(2,1)S(1)} custom-call(bf16[8,64,512]{2,1,0:T(8,128)(2,1)S(1)} %bitcast.5, bf16[16,8,32,1024]{3,2,1,0:T(8,128)(2,1)} %get-tuple-element.12.w_ref), custom_call_target="tpu_custom_call" | custom-call | flops 4294967296 | bytes 100000000 | tf_op jit(solution)/shard_map/pallas_call | solution.py:775
  165.2 1.0 copy.10
Async XLA Ops:
  108.3 1.0 copy-start

commit v5 on v4

--- a/solution.py
+++ b/solution.py
@@ -271,8 +271,10 @@
             self.arrived("z down")
             self.arrived("far")
 
+    def last(self):
+        self.arrived("z far")
+
     def end(self):
-        self.arrived("z far")
         for i, name in enumerate(self.piece):
             self.wait(self.near_piece[name], 7 + i)
         for copy in self.started:
@@ -620,8 +622,9 @@
     gather.run(use, done, columns.step)
     shared.pass_on(0)
     shared.pass_on(1)
+    columns.last()
+    shared.pass_on(2)
     columns.end()
-    shared.pass_on(2)
     shared.end()
     gather.end()
 
@@ -700,9 +703,10 @@
 
 
 def output_kernel(
-    own_ref,
+    own_hbm,
     w_ref,
     out_ref,
+    own_ref,
     buf,
     w_buf,
     total,
@@ -718,6 +722,8 @@
     part = own_ref.shape[1] // SUBS
     others = all_others(me)
     greet(others)
+    load_own = pltpu.make_async_copy(own_hbm, own_ref, own_sem.at[SUBS])
+    load_own.start()
 
     def run_of(ref, s):
         return ref.at[:, pl.ds(s * part, part)]
@@ -727,6 +733,7 @@
     for i, t in enumerate([me] + gather.owner):
         loads.append(pltpu.make_async_copy(w_ref.at[:, t], w_buf.at[i], w_sem.at[i]))
         loads[-1].start()
+    load_own.wait()
     greeted(N_T - 1)
     depth = own_ref.shape[2]
     columns = total.shape[1]
@@ -775,9 +782,10 @@
     return pl.pallas_call(
         output_kernel,
         out_shape=jax.ShapeDtypeStruct((each, columns * N_T), jnp.bfloat16),
-        in_specs=[pl.BlockSpec(memory_space=VMEM), pl.BlockSpec(memory_space=pltpu.HBM)],
+        in_specs=[pl.BlockSpec(memory_space=pltpu.HBM), pl.BlockSpec(memory_space=pltpu.HBM)],
         out_specs=pl.BlockSpec(memory_space=pltpu.HBM),
         scratch_shapes=[
+            VMEM((N_T, each, depth), jnp.bfloat16),
             VMEM((N_T, N_T, each, depth), jnp.bfloat16),
             VMEM((N_T, weight.shape[0], weight.shape[2], columns), jnp.bfloat16),
             VMEM((rows, columns), jnp.float32),
@@ -786,7 +794,7 @@
             DMA((N_T,)),
             DMA((N_T - 1, SUBS)),
             DMA((N_T - 1, SUBS)),
-            DMA((SUBS,)),
+            DMA((SUBS + 1,)),
         ],
         compiler_params=pltpu.CompilerParams(
             collective_id=3, has_side_effects=True, vmem_limit_bytes=48 * 2**20
@@ -847,13 +855,13 @@
         low_tile = lax.div(starts[0, a * TILE_Q], TILE_K)
         high_tile = lax.div(base + TILE_Q, TILE_K)
 
-        def one(i, carry, a=a, start=start, query_row=query_row, high_tile=high_tile):
-            tile = high_tile - 1 - i
+        def one(tile, carry, masked, a=a, start=start, query_row=query_row):
             cut = pl.ds(pl.multiple_of(tile * TILE_K, TILE_K), TILE_K)
             keys = kv_ref[cut, :HD]
             values = kv_ref[cut, HD:].T
-            key_row = tile * TILE_K + lax.broadcasted_iota(jnp.int32, (TILE_K, TILE_Q), 0)
-            allowed = (key_row >= start) & (key_row <= query_row)
+            if masked:
+                key_row = tile * TILE_K + lax.broadcasted_iota(jnp.int32, (TILE_K, TILE_Q), 0)
+                allowed = (key_row >= start) & (key_row <= query_row)
             after = []
             for h in range(heads):
                 top, denominator, weighted = carry[h]
@@ -861,7 +869,9 @@
                 scores = lax.dot_general(
                     keys, query, (((1,), (1,)), ((), ())), preferred_element_type=jnp.float32
                 )
-                scores = jnp.where(allowed, scores * factor, 2 * LOW)
+                scores = scores * factor
+                if masked:
+                    scores = jnp.where(allowed, scores, 2 * LOW)
                 new_top = jnp.maximum(top, jnp.max(scores, axis=0, keepdims=True))
                 weights = jnp.exp2(scores - new_top)
                 shrink = jnp.exp2(top - new_top)
@@ -874,12 +884,19 @@
                 after.append((new_top, denominator, weighted))
             return tuple(after)
 
+        full_tile = jnp.minimum(
+            lax.div(starts[0, (a + 1) * TILE_Q - 1] + TILE_K - 1, TILE_K), high_tile - 1
+        )
         begin = (
             jnp.full((1, TILE_Q), LOW, jnp.float32),
             jnp.zeros((1, TILE_Q), jnp.float32),
             jnp.zeros((HD, TILE_Q), jnp.float32),
         )
-        ended = lax.fori_loop(0, high_tile - low_tile, one, (begin,) * heads)
+        ended = one(high_tile - 1, (begin,) * heads, True)
+        ended = lax.fori_loop(
+            full_tile, high_tile - 1, lambda t, carry: one(t, carry, False), ended
+        )
+        ended = lax.fori_loop(low_tile, full_tile, lambda t, carry: one(t, carry, True), ended)
         for h in range(heads):
             _, denominator, weighted = ended[h]
             out_ref[a * TILE_Q : (a + 1) * TILE_Q, h * HD : (h + 1) * HD] = (

time: 166 us -> 163 us (0.982)
  Pallas kernels: 164 us -> 162 us
    pallas_call x1, Pallas kernels: 55.8 us -> 52.1 us  [project_out(): pl.pallas_call(output_kernel, out_shape=jax.ShapeDtypeStruct((each, colum...]
    pallas_call x1, Pallas kernels: 6.38 us -> 8.98 us  [attend(): pl.pallas_call(attend_kernel, out_shape=jax.ShapeDtypeStruct(queries.shap...]
where the time goes in v5:
time: 163 us; the launch traced here: 164 us
  Pallas kernels  162 us (99%)
  local copies, waits for them, and re-layouts  2.01 us (1%)
    pallas_call x1, Pallas kernels, project(): pl.pallas_call(project_kernel, out_shape=(jax.ShapeDtypeStruct((rows, GRO...  101 us
    pallas_call x1, Pallas kernels, project_out(): pl.pallas_call(output_kernel, out_shape=jax.ShapeDtypeStruct((each, colum...  52.1 us
    pallas_call x1, Pallas kernels, attend(): pl.pallas_call(attend_kernel, out_shape=jax.ShapeDtypeStruct(queries.shap...  8.98 us

profile of v5, /device:TPU:32, one launch (start us, length us, event | category | flops | bytes accessed | tf_op | source)
XLA Modules:
  0.0 164.0 jit_solution(533901686322409694)
XLA Ops:
  0.0 100.8 %shard_map.82 = (bf16[512,512]{1,0:T(8,128)(2,1)}, s32[8,512]{1,0:T(8,128)}, bf16[16,512,256]{2,1,0:T(8,128)(2,1)}, bf16[16,8,32,1024]{3,2,1,0:T(8,128)(2,1)}) custom-call(bf16[512,1024]{1,0:T(8,128)(2,1)} %tok_hbm.1, f32[8,1,1024]{2,1,0:T(1,128)} %bitcast.7, s32[1,512]{1,0:T(1,128)} %bitcast.8, s32[1,512]{1,0:T(1,128)} %bitcast.9, ...), custom_call_target="tpu_custom_call" | custom-call | flops 6442450944 | bytes 100000000 | tf_op jit(solution)/shard_map/pallas_call | solution.py:641
  100.9 9.0 %shard_map.83 = bf16[512,512]{1,0:T(8,128)(2,1)} custom-call(s32[8,512]{1,0:T(8,128)} %get-tuple-element.9.spots_hbm, bf16[512,512]{1,0:T(8,128)(2,1)} %get-tuple-element.10.q_hbm, bf16[16,512,256]{2,1,0:T(8,128)(2,1)} %get-tuple-element.11.kv_hbm), custom_call_target="tpu_custom_call" | custom-call | flops 1000000000 | bytes 10000000 | tf_op jit(solution)/shard_map/pallas_call | solution.py:910
  109.8 0.0 copy-start
  109.9 1.0 copy-done
  110.9 52.1 %shard_map.84 = bf16[64,8192]{1,0:T(8,128)(2,1)S(1)} custom-call(bf16[8,64,512]{2,1,0:T(8,128)(2,1)S(1)} %bitcast.5, bf16[16,8,32,1024]{3,2,1,0:T(8,128)(2,1)} %get-tuple-element.12.w_ref), custom_call_target="tpu_custom_call" | custom-call | flops 4294967296 | bytes 100000000 | tf_op jit(solution)/shard_map/pallas_call | solution.py:782
  163.0 1.0 copy.10
Async XLA Ops:
  109.8 1.0 copy-start

commit v6 on v5

--- a/solution.py
+++ b/solution.py
@@ -128,9 +128,9 @@
             self.wait(3, s)
             self.forward(3, 6, s, self.pair)
             use(3, s)
-            between(s)
             if s > 0:
                 self.last(s - 1, use, done)
+            between(s)
         self.across_sides(SUBS - 1, use)
         self.last(SUBS - 1, use, done)
 

time: 163 us -> 165 us (1.012)
    pallas_call x1, Pallas kernels: 101 us -> 103 us  [project(): pl.pallas_call(project_kernel, out_shape=(jax.ShapeDtypeStruct((rows, GRO...]
    pallas_call x1, Pallas kernels: 8.98 us -> 7.29 us  [attend(): pl.pallas_call(attend_kernel, out_shape=jax.ShapeDtypeStruct(queries.shap...]
where the time goes in v6:
time: 165 us; the launch traced here: 164 us
  Pallas kernels  162 us (98%)
  local copies, waits for them, and re-layouts  2.01 us (1%)
    pallas_call x1, Pallas kernels, project(): pl.pallas_call(project_kernel, out_shape=(jax.ShapeDtypeStruct((rows, GRO...  103 us
    pallas_call x1, Pallas kernels, project_out(): pl.pallas_call(output_kernel, out_shape=jax.ShapeDtypeStruct((each, colum...  52.3 us
    pallas_call x1, Pallas kernels, attend(): pl.pallas_call(attend_kernel, out_shape=jax.ShapeDtypeStruct(queries.shap...  7.29 us

profile of v6, /device:TPU:32, one launch (start us, length us, event | category | flops | bytes accessed | tf_op | source)
XLA Modules:
  0.0 164.4 jit_solution(153873604301569901)
XLA Ops:
  0.0 102.7 %shard_map.82 = (bf16[512,512]{1,0:T(8,128)(2,1)}, s32[8,512]{1,0:T(8,128)}, bf16[16,512,256]{2,1,0:T(8,128)(2,1)}, bf16[16,8,32,1024]{3,2,1,0:T(8,128)(2,1)}) custom-call(bf16[512,1024]{1,0:T(8,128)(2,1)} %tok_hbm.1, f32[8,1,1024]{2,1,0:T(1,128)} %bitcast.7, s32[1,512]{1,0:T(1,128)} %bitcast.8, s32[1,512]{1,0:T(1,128)} %bitcast.9, ...), custom_call_target="tpu_custom_call" | custom-call | flops 6442450944 | bytes 100000000 | tf_op jit(solution)/shard_map/pallas_call | solution.py:641
  102.7 7.3 %shard_map.83 = bf16[512,512]{1,0:T(8,128)(2,1)} custom-call(s32[8,512]{1,0:T(8,128)} %get-tuple-element.9.spots_hbm, bf16[512,512]{1,0:T(8,128)(2,1)} %get-tuple-element.10.q_hbm, bf16[16,512,256]{2,1,0:T(8,128)(2,1)} %get-tuple-element.11.kv_hbm), custom_call_target="tpu_custom_call" | custom-call | flops 1000000000 | bytes 10000000 | tf_op jit(solution)/shard_map/pallas_call | solution.py:910
  110.0 0.0 copy-start
  110.0 1.0 copy-done
  111.0 52.3 %shard_map.84 = bf16[64,8192]{1,0:T(8,128)(2,1)S(1)} custom-call(bf16[8,64,512]{2,1,0:T(8,128)(2,1)S(1)} %bitcast.5, bf16[16,8,32,1024]{3,2,1,0:T(8,128)(2,1)} %get-tuple-element.12.w_ref), custom_call_target="tpu_custom_call" | custom-call | flops 4294967296 | bytes 100000000 | tf_op jit(solution)/shard_map/pallas_call | solution.py:782
  163.4 1.0 copy.10
Async XLA Ops:
  110.0 1.0 copy-start
